TPU v7x, 256 devices: a whole 4x4x8 slice. The times are simulated.
256 devices in a mesh: row: 32 (over z, x), col: 8 (over y, core).
Axes of the slice: x: 4, y: 4, z: 8, core: 2. Of those that a mesh axis runs over, the one named last changes fastest.
Arguments:
- acts: bfloat16 [4096, 28672], P('col', 'row'), may hold values from -450 to 450
- out_grads: bfloat16 [4096, 8192], P('row', 'col'), may hold values from -150 to 150
- moment: float32 [28672, 8192], P('row', 'col'), may hold values from -6 to 6
- row_state: float32 [28672], P('row'), may hold values from 0.2 to 3
- col_state: float32 [8192], P('col'), may hold values from 0.2 to 3
- row_conf: float32 [28672], P('row'), may hold values from 0.2 to 2
- col_conf: float32 [8192], P('col'), may hold values from 0.2 to 2
Outputs:
- moment_new: float32 [28672, 8192], P('row', 'col')
- update: float32 [28672, 8192], P('row', 'col')
- row_new: float32 [28672], P('row')
- col_new: float32 [8192], P('col')
- row_conf_new: float32 [28672], P('row')
- col_conf_new: float32 [8192], P('col')
All inputs are finite; a program needn't handle non-finite values.
Results may differ from a plain program's by a relative error of at most 0.0003.
Values may be sent and summed in bfloat16 or wider, within the bound.
A program may use at most 128 MiB of HBM per device.

v0:
```python
import math

import jax
import jax.numpy as jnp
from jax import lax
from jax.sharding import PartitionSpec as P

STEP = 10


first_decay = 0.9
tiny_moment = 1e-30
tiny_confidence = 1e-16


def contract_tokens(left, right):
    return lax.dot_general(
        left, right, (((0,), (0,)), ((), ())), preferred_element_type=jnp.float32
    )


def on_device(acts, out_grads, moment, row_state, col_state, row_conf, col_conf):
    local_rows = moment.shape[0]
    local_cols = moment.shape[1]
    full_rows = local_rows * lax.axis_size("row")
    full_cols = local_cols * lax.axis_size("col")
    act_panel = lax.all_gather(acts, "col", axis=0, tiled=True)
    gradient = contract_tokens(act_panel, lax.all_gather(out_grads, "row", axis=0, tiled=True))
    squares = gradient * gradient
    second_decay = 1.0 - STEP ** (-0.8)
    norm_bound = math.sqrt(full_rows * full_cols)
    overall = lax.psum(jnp.sum(squares), ("row", "col"))
    scaling = jnp.minimum(1.0, norm_bound / jnp.sqrt(overall + 1e-06))
    squared = scaling * scaling * squares + tiny_moment
    row_sums = lax.psum(jnp.sum(squared, axis=1), "col")
    row_new = second_decay * row_state + (1.0 - second_decay) * (row_sums / full_cols)
    col_sums, row_factor_sum = lax.psum((jnp.sum(squared, axis=0), jnp.sum(row_new)), "row")
    col_new = second_decay * col_state + (1.0 - second_decay) * (col_sums / full_rows)
    row_mean = row_factor_sum / full_rows
    factored = row_new[:, None] * col_new[None, :] / row_mean
    direction = scaling * gradient / jnp.sqrt(factored)
    moment_new = first_decay * moment + (1.0 - first_decay) * direction
    unsteady = (direction - moment_new) ** 2 + tiny_confidence
    unsteady_rows = lax.psum(jnp.sum(unsteady, axis=1), "col")
    row_conf_new = second_decay * row_conf + (1.0 - second_decay) * (unsteady_rows / full_cols)
    unsteady_cols, conf_sum = lax.psum((jnp.sum(unsteady, axis=0), jnp.sum(row_conf_new)), "row")
    col_conf_new = second_decay * col_conf + (1.0 - second_decay) * (unsteady_cols / full_rows)
    confident = row_conf_new[:, None] * col_conf_new[None, :] / (conf_sum / full_rows)
    update = moment_new / jnp.sqrt(confident)
    return (moment_new, update, row_new, col_new, row_conf_new, col_conf_new)


def solution(mesh):
    placed = (
        P("col", "row"),
        P("row", "col"),
        P("row", "col"),
        P("row"),
        P("col"),
        P("row"),
        P("col"),
    )
    return jax.shard_map(
        on_device,
        mesh=mesh,
        in_specs=placed,
        out_specs=(P("row", "col"), P("row", "col"), P("row"), P("col"), P("row"), P("col")),
        check_vma=False,
    )
```

profile of v0, /device:TPU:2, one launch (start us, length us, event | category | flops | bytes accessed | tf_op | source)
XLA Modules:
  0.0 444.0 jit_solution(9726992637784641175)
XLA Ops:
  7.2 0.0 all-gather.3.cloned.1.call-start
  7.2 0.7 all-gather.3.cloned.1.call-update
  7.9 0.0 all-gather.5.cloned.1.call-start
  7.9 0.7 all-gather.5.cloned.1.call-update
  8.6 52.1 %all-gather.3.cloned.1.call-done = bf16[4096,896]{1,0:T(8,128)(2,1)} async-done(((bf16[512,896]{1,0:T(8,128)(2,1)}), bf16[4096,896]{1,0:T(8,128)(2,1)}) %all-gather.3.cloned.1.call-update) | async-done | bytes 7340048 | tf_op jit(solution)/shard_map/all_gather | solution.py:27
  60.7 99.8 %all-gather.5.cloned.1.call-done = bf16[4096,1024]{1,0:T(8,128)(2,1)} async-done(((bf16[128,1024]{1,0:T(8,128)(2,1)}), bf16[4096,1024]{1,0:T(8,128)(2,1)}) %all-gather.5.cloned.1.call-update) | async-done | bytes 8388624 | tf_op jit(solution)/shard_map/all_gather | solution.py:28
  160.5 14.4 %multiply_reduce_fusion = (f32[]{:T(128)}, f32[896,1024]{1,0:T(8,128)}) fusion(bf16[4096,896]{1,0:T(8,128)(2,1)} %all-gather.3.cloned.1.call-done, bf16[4096,1024]{1,0:T(8,128)(2,1)} %all-gather.5.cloned.1.call-done), kind=kOutput, calls=%fused_computation.5 | convolution fusion | flops 7518027776 | bytes 19398660 | tf_op jit(solution)/shard_map/dot_general | solution.py:17
  174.9 75.1 %psum.49 = f32[]{:T(128)} all-reduce(f32[]{:T(128)} %get-tuple-element.19), channel_id=1, replica_groups=mesh['row'=32,'col'=8] {'row','col'}, use_global_device_ids=true, to_apply=%region_1.0 | all-reduce | flops 1 | bytes 8 | tf_op jit(solution)/shard_map/psum | solution.py:32
  250.7 2.8 fusion
  253.5 13.1 %psum.50 = f32[896]{0:T(1024)S(1)} all-reduce(f32[896]{0:T(1024)S(1)} %get-tuple-element.9), channel_id=1, replica_groups=mesh['row'=32,'col'=8] {'col'}, use_global_device_ids=true, to_apply=%region_3.0 | all-reduce | flops 896 | bytes 7168 | tf_op jit(solution)/shard_map/psum | solution.py:35
  266.6 0.0 copy-done.4
  266.6 0.6 fusion.5
  267.2 73.3 %all-reduce.1 = (f32[]{:T(128)}, f32[1024]{0:T(1024)S(1)}) all-reduce(f32[]{:T(128)} %get-tuple-element.17, f32[1024]{0:T(1024)S(1)} %get-tuple-element.8), channel_id=1, replica_groups=mesh['row'=32,'col'=8] {'row'}, use_global_device_ids=true, to_apply=%region_7.0 | all-reduce | flops 1025 | bytes 8200 | tf_op jit(solution)/shard_map/psum | solution.py:37
  341.2 0.0 copy-done.5
  341.2 0.0 copy-start.1
  341.2 0.0 copy-start.6
  341.2 0.0 copy-start.7
  341.2 5.3 %fusion.2 = (f32[1024]{0:T(1024)S(1)}, f32[896]{0:T(1024)S(1)}, f32[896,1024]{1,0:T(8,128)}) fusion(f32[]{:T(128)S(6)} %div.32, f32[1024]{0:T(1024)S(1)} %multiply_add_fusion.5, f32[896]{0:T(1024)S(1)} %get-tuple-element.18, f32[896,1024]{1,0:T(8,128)} %get-tuple-element.20, f32[]{:T(128)S(6)} %min_shard_map.3, f32[896,1024]{1,0:T(8,128)} %param.9), kind=kLoop, calls=%fused_computation.8 | loop fusion | flops 11008128 | bytes 11025416 | tf_op jit(solution)/shard_map/reduce_sum | solution.py:46
  346.6 12.4 %psum.53 = f32[896]{0:T(1024)S(1)} all-reduce(f32[896]{0:T(1024)S(1)} %get-tuple-element.7), channel_id=1, replica_groups=mesh['row'=32,'col'=8] {'col'}, use_global_device_ids=true, to_apply=%region_9.0 | all-reduce | flops 896 | bytes 7168 | tf_op jit(solution)/shard_map/psum | solution.py:44
  359.0 0.6 fusion.4
  359.6 72.4 %all-reduce = (f32[]{:T(128)}, f32[1024]{0:T(1024)S(1)}) all-reduce(f32[]{:T(128)} %get-tuple-element.14, f32[1024]{0:T(1024)S(1)} %get-tuple-element.6), channel_id=1, replica_groups=mesh['row'=32,'col'=8] {'row'}, use_global_device_ids=true, to_apply=%region_13.0 | all-reduce | flops 1025 | bytes 8200 | tf_op jit(solution)/shard_map/psum | solution.py:46
  432.7 0.0 copy-start.3
  432.7 4.4 rsqrt_multiply_fusion
  437.1 0.0 copy-done.3
  (11 shorter events, 0.0 us)
Async XLA Ops:
  7.2 53.5 %all-gather.3.cloned.1.call-start = ((), (), s32[]{:S(2)}) async-start(), calls=%async_computation | async-start | bytes 8257536 | tf_op jit(solution)/shard_map/all_gather | solution.py:27
  7.9 152.6 %all-gather.5.cloned.1.call-start = ((), (), s32[]{:S(2)}) async-start(), calls=%async_computation.1 | async-start | bytes 8650752 | tf_op jit(solution)/shard_map/all_gather | solution.py:28
  174.9 91.7 %copy-start.4 = (f32[896]{0:T(1024)S(1)}, f32[896]{0:T(1024)}, u32[]{:S(2)}) copy-start(f32[896]{0:T(1024)} %param.10) | copy-start | bytes 10756
  174.9 166.2 %copy-start.5 = (f32[1024]{0:T(1024)S(1)}, f32[1024]{0:T(1024)}, u32[]{:S(2)}) copy-start(f32[1024]{0:T(1024)} %param.11) | copy-start | bytes 12292
  267.2 79.4 %copy-start = (f32[896]{0:T(1024)}, f32[896]{0:T(1024)S(1)}, u32[]{:S(2)}) copy-start(f32[896]{0:T(1024)S(1)} %get-tuple-element.18) | copy-start | bytes 10756
  341.2 5.4 %copy-start.1 = (f32[1024]{0:T(1024)}, f32[1024]{0:T(1024)S(1)}, u32[]{:S(2)}) copy-start(f32[1024]{0:T(1024)S(1)} %multiply_add_fusion.5) | copy-start | bytes 12292
  341.2 17.8 %copy-start.6 = (f32[896]{0:T(1024)S(1)}, f32[896]{0:T(1024)}, u32[]{:S(2)}) copy-start(f32[896]{0:T(1024)} %param.12) | copy-start | bytes 10756
  341.2 91.4 %copy-start.7 = (f32[1024]{0:T(1024)S(1)}, f32[1024]{0:T(1024)}, u32[]{:S(2)}) copy-start(f32[1024]{0:T(1024)} %param.13) | copy-start | bytes 12292
  359.6 77.5 %copy-start.2 = (f32[896]{0:T(1024)}, f32[896]{0:T(1024)S(1)}, u32[]{:S(2)}) copy-start(f32[896]{0:T(1024)S(1)} %get-tuple-element.15) | copy-start | bytes 10756
  432.7 4.5 %copy-start.3 = (f32[1024]{0:T(1024)}, f32[1024]{0:T(1024)S(1)}, u32[]{:S(2)}) copy-start(f32[1024]{0:T(1024)S(1)} %multiply_add_fusion.3) | copy-start | bytes 12292
Sparse Core Ops, SparseCore 0:
  9.8 50.8 all-gather.2
  63.3 97.1 all-gather.4
where the time goes:
time: 444 us
  blocking collectives  246 us (55%)
  waiting for transfers between devices  153 us (34%)
  between operations  16.1 us (4%)
  matrix products  14.4 us (3%)
  other arithmetic  13.8 us (3%)
    all_gather x1, waiting for transfers between devices, on_device(): lax.all_gather(out_grads, 'row', axis=0, tiled=True)  99.8 us
    psum x1, blocking collectives, on_device(): overall = lax.psum(jnp.sum(squares), ('row', 'col'))  75.1 us
    psum x1, blocking collectives, on_device(): lax.psum((jnp.sum(squared, axis=0), jnp.sum(row_new)), 'row')  73.3 us
    psum x1, blocking collectives, on_device(): lax.psum((jnp.sum(unsteady, axis=0), jnp.sum(row_conf_new)), 'row')  72.4 us
    all_gather x1, waiting for transfers between devices, on_device(): act_panel = lax.all_gather(acts, 'col', axis=0, tiled=True)  52.1 us
    dot_general x1, matrix products, contract_tokens(): lax.dot_general(left, right, (((0,), (0,)), ((), ())), preferred_element_...  14.4 us
    psum x1, blocking collectives, on_device(): row_sums = lax.psum(jnp.sum(squared, axis=1), 'col')  13.1 us
    psum x1, blocking collectives, on_device(): unsteady_rows = lax.psum(jnp.sum(unsteady, axis=1), 'col')  12.4 us
  transfers between devices with their start and end apart: 2, of which 2 were waited for; matrix products, arithmetic and copies ran while one was open for 0% of the time, Pallas kernels for 0%

commit v1 on v0

v1 whole, which is shorter than its diff:
```python
import functools

import jax
import jax.numpy as jnp
from jax import lax
from jax.experimental import pallas as pl
from jax.experimental.pallas import tpu as pltpu
from jax.sharding import PartitionSpec as P

MESH = pl.DeviceIdType.MESH
F32 = jnp.float32
STEP = 10
X = 4
LANES = 128

first_decay = 0.9
tiny_moment = 1e-30
tiny_confidence = 1e-16
second_decay = 1.0 - STEP ** (-0.8)


def kernel(R, C, acts, grads, moment, row_state, col_state, row_conf, col_conf,
           moment_out, update_out, row_out, col_out, row_conf_out, col_conf_out,
           A, B, G, M, states, row_part, row_got, col_part, col_got, tot_part, tot_got,
           ring_send, ring_recv, act_send, act_recv, load_sem, store_sem,
           row_send, row_recv, col_send, col_recv, tot_send, tot_recv):
    Z, Y = R // X, C // 2
    row, col = lax.axis_index("row"), lax.axis_index("col")
    div, rem = lax.div, lax.rem
    z, x, y, core = div(row, X), rem(row, X), div(col, 2), rem(col, 2)
    tb, shard = grads.shape[0], acts.shape[0]
    half, chunk, hs = tb // 2, tb // 4, shard // 2
    rows, cols = G.shape
    nr, nc = rows // LANES, cols // LANES
    full_rows, full_cols = rows * R, cols * C
    S = R // 2
    near_step, far_step = 7 * S // 16, 10 * S // 16

    def cycle0(t):
        t = rem(t, R)
        u, v = div(t, X), rem(t, X)
        return u * X + rem(v + 3 * u, X)

    def cycle1(t):
        t = rem(t, R)
        u, v = div(t, X), rem(t, X)
        return rem(3 * u + v, Z) * X + rem(u, X)

    p0 = z * X + rem(x + z, X)
    w = rem(z + (3 * Z - 3) * x, Z)
    p1 = X * (x + X * div(w, X)) + rem(w, X)

    def origin(lane, k):
        cycle, p = ((cycle0, p0), (cycle1, p1))[lane // 2]
        return cycle(p - k + R) if lane % 2 == 0 else cycle(p + k + R)

    def part(first, unit, size):
        return pl.ds(pl.multiple_of(first, unit), size)

    ring_to = [origin(lane, -1) for lane in range(4)]
    up, down = rem(y + 1, Y) * 2 + core, rem(y + Y - 1, Y) * 2 + core
    far, twin = rem(y + 2, Y) * 2 + core, y * 2 + 1 - core

    barrier = pltpu.get_barrier_semaphore()
    for r in ring_to:
        pl.semaphore_signal(barrier, inc=1, device_id=(r, col), device_id_type=MESH)
    for c in (up, down, twin):
        pl.semaphore_signal(barrier, inc=1, device_id=(row, c), device_id_type=MESH)

    loads = [
        pltpu.make_async_copy(grads, B.at[part(row * tb, tb, tb)], load_sem.at[0]),
        pltpu.make_async_copy(acts, A.at[part(col * shard, shard, shard)], load_sem.at[1]),
        pltpu.make_async_copy(moment, M, load_sem.at[2]),
        pltpu.make_async_copy(row_state, states.at[0, pl.ds(0, nr)], load_sem.at[3]),
        pltpu.make_async_copy(col_state, states.at[1, pl.ds(0, nc)], load_sem.at[4]),
        pltpu.make_async_copy(row_conf, states.at[2, pl.ds(0, nr)], load_sem.at[5]),
        pltpu.make_async_copy(col_conf, states.at[3, pl.ds(0, nc)], load_sem.at[6]),
    ]
    states[...] = jnp.zeros_like(states)
    for load in loads:
        load.start()
    pl.semaphore_wait(barrier, 7)

    def ring(lane, s, q, k):
        rows_k = part(origin(lane, k) * tb + (lane // 2) * half + q * chunk, chunk, chunk)
        return pltpu.make_async_remote_copy(
            src_ref=B.at[rows_k], dst_ref=B.at[rows_k],
            send_sem=ring_send.at[lane, 2 * s + q], recv_sem=ring_recv.at[lane, 2 * s + q],
            device_id=(ring_to[lane], col), device_id_type=MESH)

    def ring_first(lane, q):
        first = (lane // 2) * half + q * chunk
        return pltpu.make_async_remote_copy(
            src_ref=grads.at[pl.ds(first, chunk)],
            dst_ref=B.at[part(row * tb + first, chunk, chunk)],
            send_sem=ring_send.at[lane, q], recv_sem=ring_recv.at[lane, q],
            device_id=(ring_to[lane], col), device_id_type=MESH)

    def ring_out(lane, s, q):
        return ring(lane, s, q, s)

    def ring_in(lane, s, q):
        return ring(lane, s, q, s + 1)

    def act(i, owner, first, size, to, src=None):
        there = A.at[part(owner * shard + first, hs, size)]
        return pltpu.make_async_remote_copy(
            src_ref=there if src is None else src, dst_ref=there,
            send_sem=act_send.at[i], recv_sem=act_recv.at[i],
            device_id=(row, to), device_id_type=MESH)

    low, high = acts.at[pl.ds(0, hs)], acts.at[pl.ds(hs, hs)]
    act_out = {
        0: act(0, col, 0, hs, up, low), 3: act(3, col, hs, hs, down, high),
        1: act(1, col, hs, hs, up, high), 4: act(4, col, 0, hs, down, low),
        6: act(6, col, 0, shard, twin, acts),
        2: act(2, down, 0, hs, up), 5: act(5, up, hs, hs, down),
        7: act(7, down, 0, shard, twin), 8: act(8, up, 0, shard, twin),
        9: act(9, far, 0, hs, twin), 10: act(10, far, hs, hs, twin),
    }
    swap = 1 - 2 * core
    act_in = {
        0: act(0, down, 0, hs, up), 1: act(1, down, hs, hs, up), 2: act(2, far, 0, hs, up),
        3: act(3, up, hs, hs, down), 4: act(4, up, 0, hs, down), 5: act(5, far, hs, hs, down),
        6: act(6, twin, 0, shard, twin), 7: act(7, down + swap, 0, shard, twin),
        8: act(8, up + swap, 0, shard, twin), 9: act(9, far + swap, 0, hs, twin),
        10: act(10, far + swap, hs, hs, twin),
    }

    for q in range(2):
        for lane in range(4):
            ring_first(lane, q).start()
    for i in (0, 3, 1, 4, 6):
        act_out[i].start()

    def product(firsts):
        a = jnp.concatenate([A[part(f, half, half), :] for f in firsts], 0)
        b = jnp.concatenate([B[part(f, half, half), :] for f in firsts], 0)
        return lax.dot_general(a, b, (((0,), (0,)), ((), ())), preferred_element_type=F32)

    def hop(s, q):
        for lane in range(4):
            ring_in(lane, s, q).wait_recv()
            ring_out(lane, s + 1, q).start()

    def hops(first, last):
        def both(s, carry):
            hop(s, 0)
            hop(s, 1)
            return carry
        lax.fori_loop(first, last, both, 0)

    def add_units(first, last):
        def add(k, carry):
            G[...] += product([origin(lane, k) * tb + (lane // 2) * half for lane in range(4)])
            return carry
        lax.fori_loop(first, last, add, 0)

    loads[0].wait()
    loads[1].wait()
    G[...] = jnp.zeros_like(G)
    hops(0, near_step)
    for i in (0, 3, 1, 4):
        act_in[i].wait_recv()
    for i in (2, 5, 7, 8):
        act_out[i].start()
    hops(near_step, far_step)
    for i in (2, 5):
        act_in[i].wait_recv()
    for i in (9, 10):
        act_out[i].start()
    hops(far_step, far_step + 1)
    for i in (6, 7, 8, 9, 10):
        act_in[i].wait_recv()

    slots = 2 * (S - 2 - far_step)
    done = 1
    for slot in range(slots):
        s, q = far_step + 1 + slot // 2, slot % 2
        if s < S - 2:
            hop(s, q)
        else:
            for lane in range(4):
                ring_in(lane, s, q).wait_recv()
                if q == lane % 2:
                    ring_out(lane, S - 1, q).start()
        upto = min(1 + (S - 1) * (slot + 1) // slots, s + 1 + q)
        add_units(done, upto)
        done = upto
    add_units(done, S)
    for lane in range(4):
        ring_in(lane, S - 1, lane % 2).wait_recv()
    G[...] += product([row * tb, row * tb + half,
                       cycle0(p0 + S) * tb, cycle1(p1 + S) * tb + half])
    for load in loads[2:]:
        load.wait()

    def exchange(phase, src, got, size, me, along, send_sem, recv_sem):
        def copy(i, slot):
            to = rem(me + i, size)
            return pltpu.make_async_remote_copy(
                src_ref=src, dst_ref=got.at[phase, slot],
                send_sem=send_sem.at[phase, i], recv_sem=recv_sem.at[phase, i],
                device_id=(to, col) if along == "row" else (row, to), device_id_type=MESH)

        def start():
            got[phase, me] = src[...]
            for i in range(1, size):
                copy(i, me).start()

        def result():
            for i in range(1, size):
                copy(i, rem(me + size - i, size)).wait_recv()
            return jnp.sum(got[phase], axis=0)

        def drain():
            for i in range(1, size):
                copy(i, me).wait_send()

        return start, result, drain

    def whole(tile):
        return jnp.sum(tile, axis=(0, 1), keepdims=True)

    def sums(phase, block):
        def rows_of(i, col_sum):
            at = part(i * LANES, LANES, LANES)
            row_sum = jnp.zeros((LANES, LANES), F32)
            col_sums = []
            for j in range(nc):
                square = block(i, at, j)
                row_sum += square
                col_sums.append(jnp.sum(square.reshape(LANES // 8, 8, LANES), axis=0))
            row_part[phase, pl.ds(i, 1), :] = jnp.sum(row_sum.T, axis=0, keepdims=True)
            return col_sum + jnp.concatenate(col_sums, 1)

        col_sum = lax.fori_loop(0, nr, rows_of, jnp.zeros((8, cols), F32))
        col_sum = jnp.sum(col_sum, axis=0, keepdims=True)
        for j in range(nc):
            col_part[phase, j:j + 1, :] = col_sum[:, j * LANES:(j + 1) * LANES]

    def reduced(phase, meanwhile):
        by_col = exchange(phase, col_part.at[phase], col_got, R, row, "row", col_send, col_recv)
        by_row = exchange(phase, row_part.at[phase], row_got, C, col, "col", row_send, row_recv)
        by_col[0]()
        by_row[0]()
        meanwhile()
        col_all = by_col[1]()
        tot_part[phase] = col_all[0:8, :]
        by_tot = exchange(phase, tot_part.at[phase], tot_got, C, col, "col", tot_send, tot_recv)
        by_tot[0]()
        row_all = by_row[1]()
        total = whole(by_tot[1]())

        def drain():
            for one in (by_col, by_row, by_tot):
                one[2]()
        return row_all, col_all, total, drain

    def down_rows(factor_ref, i):
        return jnp.broadcast_to(factor_ref[pl.ds(i, 1), :], (LANES, LANES)).T

    col_part[...] = jnp.zeros_like(col_part)
    row_part[...] = jnp.zeros_like(row_part)
    col_part[0, 8:9, :] = jnp.sum(states[0], axis=0, keepdims=True)
    col_part[0, 9:10, :] = jnp.sum(states[2], axis=0, keepdims=True)

    def squared(i, at, j):
        g = G[at, j * LANES:(j + 1) * LANES]
        return g * g

    def ring_drain():
        def wait(s, carry):
            for q in range(2):
                for lane in range(4):
                    ring_out(lane, s, q).wait_send()
            return carry
        lax.fori_loop(0, S - 1, wait, 0)
        for lane in range(4):
            ring_out(lane, S - 1, lane % 2).wait_send()
        for copy in act_out.values():
            copy.wait_send()

    sums(0, squared)
    row_all, col_all, total, drain0 = reduced(0, ring_drain)
    scaling = jnp.minimum(1.0, (full_rows * full_cols) ** 0.5 / jnp.sqrt(total + 1e-06))
    keep, fresh = second_decay, 1.0 - second_decay
    spread = scaling * scaling
    row_new = keep * states[0] + fresh * (spread * row_all * (1.0 / full_cols) + tiny_moment)
    col_new = keep * states[1] + fresh * (spread * col_all[0:8, :] * (1.0 / full_rows) + tiny_moment)
    row_mean = keep * (whole(col_all[8:9, :]) * (1.0 / full_rows)) + fresh * (
        spread * total * (1.0 / (full_rows * full_cols)) + tiny_moment)
    row_conf_sum = whole(col_all[9:10, :])
    states[0] = row_new
    states[1] = col_new
    row_part[2] = lax.rsqrt(row_new)
    col_scale = lax.rsqrt(col_new) * (scaling * jnp.sqrt(row_mean))

    def strays(i, at, j):
        here = (at, slice(j * LANES, (j + 1) * LANES))
        direction = G[here] * down_rows(row_part.at[2], i) * col_scale[j:j + 1, :]
        stray = direction - M[here]
        M[here] = M[here] + (1.0 - first_decay) * stray
        return stray * stray

    sums(1, strays)
    stores = [
        pltpu.make_async_copy(M, moment_out, store_sem.at[0]),
        pltpu.make_async_copy(states.at[0, pl.ds(0, nr)], row_out, store_sem.at[1]),
        pltpu.make_async_copy(states.at[1, pl.ds(0, nc)], col_out, store_sem.at[2]),
    ]

    def store_first():
        for store in stores:
            store.start()
        drain0()

    row_all, col_all, total, drain1 = reduced(1, store_first)
    share = first_decay * first_decay
    row_conf_new = keep * states[2] + fresh * (row_all * (share / full_cols) + tiny_confidence)
    col_conf_new = keep * states[3] + fresh * (col_all[0:8, :] * (share / full_rows) + tiny_confidence)
    conf_mean = keep * (row_conf_sum * (1.0 / full_rows)) + fresh * (
        total * (share / (full_rows * full_cols)) + tiny_confidence)
    states[2] = row_conf_new
    states[3] = col_conf_new
    stores += [
        pltpu.make_async_copy(states.at[2, pl.ds(0, nr)], row_conf_out, store_sem.at[3]),
        pltpu.make_async_copy(states.at[3, pl.ds(0, nc)], col_conf_out, store_sem.at[4]),
    ]
    for store in stores[3:]:
        store.start()
    row_part[3] = lax.rsqrt(row_conf_new)
    conf_scale = lax.rsqrt(col_conf_new) * jnp.sqrt(conf_mean)

    def update_store(i):
        at = part(i * LANES, LANES, LANES)
        return pltpu.make_async_copy(G.at[at], update_out.at[at], store_sem.at[5 + i])

    def finish(i, carry):
        at = part(i * LANES, LANES, LANES)
        scale = down_rows(row_part.at[3], i)
        for j in range(nc):
            here = (at, slice(j * LANES, (j + 1) * LANES))
            G[here] = M[here] * scale * conf_scale[j:j + 1, :]
        update_store(i).start()
        return carry

    lax.fori_loop(0, nr, finish, 0)
    drain1()
    for store in stores:
        store.wait()

    def stored(i, carry):
        update_store(i).wait()
        return carry

    lax.fori_loop(0, nr, stored, 0)


def on_device(acts, out_grads, moment, row_state, col_state, row_conf, col_conf):
    R, C = lax.axis_size("row"), lax.axis_size("col")
    rows, cols = moment.shape
    nr, nc = rows // LANES, cols // LANES
    dma = pltpu.SemaphoreType.DMA
    big = jax.ShapeDtypeStruct((rows, cols), F32)
    by_row, by_col = (jax.ShapeDtypeStruct((n, LANES), F32) for n in (nr, nc))
    anywhere = pl.BlockSpec(memory_space=pl.ANY)
    tokens = R * out_grads.shape[0]
    outs = pl.pallas_call(
        functools.partial(kernel, R, C),
        out_shape=(big, big, by_row, by_col, by_row, by_col),
        in_specs=[anywhere] * 7,
        out_specs=(anywhere,) * 6,
        scratch_shapes=[
            pltpu.VMEM((tokens, rows), acts.dtype),
            pltpu.VMEM((tokens, cols), out_grads.dtype),
            pltpu.VMEM((rows, cols), F32),
            pltpu.VMEM((rows, cols), F32),
            pltpu.VMEM((4, 8, LANES), F32),
            pltpu.VMEM((4, 8, LANES), F32),
            pltpu.VMEM((2, C, 8, LANES), F32),
            pltpu.VMEM((2, 16, LANES), F32),
            pltpu.VMEM((2, R, 16, LANES), F32),
            pltpu.VMEM((2, 8, LANES), F32),
            pltpu.VMEM((2, C, 8, LANES), F32),
            dma((4, R)), dma((4, R)), dma((11,)), dma((11,)), dma((7,)), dma((5 + nr,)),
            dma((2, C)), dma((2, C)), dma((2, R)), dma((2, R)), dma((2, C)), dma((2, C)),
        ],
        compiler_params=pltpu.CompilerParams(
            collective_id=0, has_side_effects=True, vmem_limit_bytes=48 * 2**20),
        cost_estimate=pl.CostEstimate(
            flops=2 * tokens * rows * cols, transcendentals=0, bytes_accessed=30 * 2**20),
        name="came_step",
    )(acts, out_grads, moment, row_state.reshape(nr, LANES), col_state.reshape(nc, LANES),
      row_conf.reshape(nr, LANES), col_conf.reshape(nc, LANES))
    return outs[0], outs[1], *(out.reshape(-1) for out in outs[2:])


def solution(mesh):
    placed = (
        P("col", "row"),
        P("row", "col"),
        P("row", "col"),
        P("row"),
        P("col"),
        P("row"),
        P("col"),
    )
    return jax.shard_map(
        on_device,
        mesh=mesh,
        in_specs=placed,
        out_specs=(P("row", "col"), P("row", "col"), P("row"), P("col"), P("row"), P("col")),
        check_vma=False,
    )
```

time: 444 us -> 123 us (0.28)
  the two profiles are of different devices: /device:TPU:2 before, /device:TPU:1 now
where the time goes in v1:
time: 123 us
  Pallas kernels  110 us (89%)
  local copies, waits for them, and re-layouts  12.4 us (10%)
    pallas_call x1, Pallas kernels, on_device(): pl.pallas_call(functools.partial(kernel, R, C), out_shape=(big, big, by_r...  110 us
    unnamed x20, local copies, waits for them, and re-layouts  12.4 us

profile of v1, /device:TPU:1, one launch (start us, length us, event | category | flops | bytes accessed | tf_op | source)
XLA Modules:
  0.0 123.1 jit_solution(10297669335101840743)
XLA Ops:
  0.6 0.0 copy-start
  0.6 1.2 copy-done
  1.8 0.0 copy-start.1
  1.8 0.9 copy-done.1
  2.8 0.0 copy-start.2
  2.8 0.7 copy-done.2
  3.5 0.0 copy-start.3
  3.5 0.7 copy-done.3
  4.1 0.0 copy-start.4
  4.1 0.7 copy-done.4
  4.8 0.0 copy-start.5
  4.8 0.7 copy-done.5
  5.5 110.0 %came_step.1 = (f32[896,1024]{1,0:T(8,128)S(1)}, f32[896,1024]{1,0:T(8,128)}, f32[7,128]{1,0:T(8,128)S(1)}, f32[8,128]{1,0:T(8,128)S(1)}, f32[7,128]{1,0:T(8,128)S(1)}, /*index=5*/f32[8,128]{1,0:T(8,128)S(1)}) custom-call(bf16[512,896]{1,0:T(8,128)(2,1)S(1)} %copy-done, bf16[128,1024]{1,0:T(8,128)(2,1)S(1)} %copy-done.1, f32[896,1024]{1,0:T(8,128)} %moment.1, ...), custom_call_target="tpu_custom_call" | custom-call | flops 7516192768 | bytes 31457280 | tf_op jit(solution)/shard_map/came_step/pallas_call | solution.py:369
  115.5 0.0 copy-start.6
  115.5 1.9 %copy.19 = f32[896,1024]{1,0:T(8,128)} copy(f32[896,1024]{1,0:T(8,128)S(1)} %get-tuple-element.24) | data formatting | bytes 7340032
  117.4 1.5 %copy-done.6 = f32[896,1024]{1,0:T(8,128)S(1)} copy-done((f32[896,1024]{1,0:T(8,128)S(1)}, f32[896,1024]{1,0:T(8,128)}, u32[]{:S(2)}) %copy-start.6) | copy-done | bytes 3670040
  118.9 1.8 %copy.20 = f32[896,1024]{1,0:T(8,128)} copy(f32[896,1024]{1,0:T(8,128)S(1)} %copy-done.6) | data formatting | bytes 7340032
  120.7 0.6 copy.21
  121.3 0.6 copy.22
  121.9 0.6 copy.23
  122.5 0.6 copy.24
Async XLA Ops:
  0.6 1.2 copy-start
  1.8 0.9 copy-start.1
  2.8 0.7 copy-start.2
  3.5 0.7 copy-start.3
  4.1 0.7 copy-start.4
  4.8 0.7 copy-start.5
  115.5 3.4 %copy-start.6 = (f32[896,1024]{1,0:T(8,128)S(1)}, f32[896,1024]{1,0:T(8,128)}, u32[]{:S(2)}) copy-start(f32[896,1024]{1,0:T(8,128)} %get-tuple-element.25) | copy-start | bytes 11010052

commit v2 on v1

v2 whole, which is shorter than its diff:
```python
import functools

import jax
import jax.numpy as jnp
from jax import lax
from jax.experimental import pallas as pl
from jax.experimental.pallas import tpu as pltpu
from jax.sharding import PartitionSpec as P

MESH = pl.DeviceIdType.MESH
F32 = jnp.float32
STEP = 10
X = 4
LANES = 128

first_decay = 0.9
tiny_moment = 1e-30
tiny_confidence = 1e-16
second_decay = 1.0 - STEP ** (-0.8)


ORDER = (
    ("z", "Q", 0, 0), ("x", "P", 0, 0), ("x", "Q", 0, 0), ("z", "P", 0, 0), "own low",
    ("z", "P", 1, 0), ("x", "P", 0, 1), ("x", "Q", 1, 0), ("z", "Q", 0, 1), "own high",
    ("x", "Q", -1, 0), ("z", "P", -1, 0), ("z", "P", 2, 0), ("x", "Q", 0, 1),
    ("z", "Q", 0, 2), ("x", "Q", 2, 0), ("z", "P", 0, 1), ("x", "Q", 1, 1), "near",
    ("z", "P", 1, 1), ("x", "Q", -2, 0), ("x", "Q", -1, 1), ("z", "Q", 0, 3), ("z", "P", -1, 1),
    ("x", "Q", 3, 0), ("z", "P", 2, 1), "cross",
    ("x", "Q", 2, 1), ("z", "P", 0, 2), ("x", "Q", -3, 0), ("z", "P", 1, 2), ("z", "P", -1, 2),
    ("x", "Q", -2, 1), ("z", "P", 2, 2), ("x", "Q", 4, 0), "far",
    ("z", "P", 0, 3), ("z", "P", 1, 3), "all", (0, 1, -1),
    ("x", "Q", 3, 1), ("z", "P", -1, 3), ("x", "Q", -3, 1), ("z", "P", 2, 3), (2, -2),
    ("x", "Q", 4, 1), (3, -3), (4,),
)
HOPS = {"z": 4, "x": 2}


def kernel(R, C, acts, grads, moment, row_state, col_state, row_conf, col_conf, M, packed,
           A, B, G, states, row_part, row_got, col_part, col_got, tot_part, tot_got,
           ring_send, ring_recv, act_send, act_recv, load_sem,
           row_send, row_recv, col_send, col_recv, tot_send, tot_recv):
    Z, Y = R // X, C // 2
    row, col = lax.axis_index("row"), lax.axis_index("col")
    div, rem = lax.div, lax.rem
    z, x, y, core = div(row, X), rem(row, X), div(col, 2), rem(col, 2)
    tb, shard = grads.shape[0], acts.shape[0]
    hs = shard // 2
    rows, cols = G.shape
    nr, nc = rows // LANES, cols // LANES
    full_rows, full_cols = rows * R, cols * C
    p_rows = 3 * tb // 8

    def at_offset(dz, dx):
        return rem(z + dz + Z, Z) * X + rem(x + dx + X, X)

    def part(first, unit, size):
        return pl.ds(pl.multiple_of(first, unit), size)

    ring_to = {("z", s): at_offset(s, 0) for s in (1, -1)} | {("x", s): at_offset(0, s) for s in (1, -1)}
    up, down = rem(y + 1, Y) * 2 + core, rem(y + Y - 1, Y) * 2 + core
    far, twin = rem(y + 2, Y) * 2 + core, y * 2 + 1 - core

    barrier = pltpu.get_barrier_semaphore()
    for r in ring_to.values():
        pl.semaphore_signal(barrier, inc=1, device_id=(r, col), device_id_type=MESH)
    for c in (up, down, twin):
        pl.semaphore_signal(barrier, inc=1, device_id=(row, c), device_id_type=MESH)

    loads = [
        pltpu.make_async_copy(grads, B.at[part(row * tb, tb, tb)], load_sem.at[0]),
        pltpu.make_async_copy(acts, A.at[part(col * shard, shard, shard)], load_sem.at[1]),
        pltpu.make_async_copy(moment, M, load_sem.at[2]),
        pltpu.make_async_copy(row_state, states.at[0, pl.ds(0, nr)], load_sem.at[3]),
        pltpu.make_async_copy(col_state, states.at[1, pl.ds(0, nc)], load_sem.at[4]),
        pltpu.make_async_copy(row_conf, states.at[2, pl.ds(0, nr)], load_sem.at[5]),
        pltpu.make_async_copy(col_conf, states.at[3, pl.ds(0, nc)], load_sem.at[6]),
    ]
    states[...] = jnp.zeros_like(states)
    for load in loads:
        load.start()
    pl.semaphore_wait(barrier, 7)

    def extent(message):
        axis, sign, kind, off, hops = message
        first, size = (0, p_rows) if kind == "P" else (p_rows, tb - p_rows)
        if hops == HOPS[axis] - 1:
            low = (size // 2 + 15) // 16 * 16
            low = size - low if off % 2 else low
            return (first, low) if sign > 0 else (first + low, size - low)
        return first, size

    def placed(message, hops):
        axis, sign, _, off, _ = message
        dz, dx = (-sign * hops, off) if axis == "z" else (off, -sign * hops)
        first, size = extent(message)
        return B.at[part(at_offset(dz, dx) * tb + first, 16, size)]

    numbers = {}

    def ring(message, hops):
        axis, sign, _, off, made = message
        lane = 2 * (axis == "x") + (sign < 0)
        number = numbers.setdefault(message, sum(m[:2] == message[:2] for m in numbers))
        first, size = extent(message)
        there = placed(message, hops)
        return pltpu.make_async_remote_copy(
            src_ref=grads.at[pl.ds(first, size)] if made == 0 and off == 0 else there, dst_ref=there,
            send_sem=ring_send.at[lane, number], recv_sem=ring_recv.at[lane, number],
            device_id=(ring_to[axis, sign], col), device_id_type=MESH)

    sent, landed = [], set()

    def await_messages(messages):
        for message in messages:
            if message not in landed:
                landed.add(message)
                ring(message, message[4] + 1).wait_recv()

    def brought(message):
        axis, sign, kind, off, hops = message
        if hops > 0:
            return [(axis, sign, kind, off, hops - 1)]
        if off == 0:
            return []
        other = "x" if axis == "z" else "z"
        last = HOPS[other] - 1
        if abs(off) == HOPS[other]:
            return [(other, 1, kind, 0, last), (other, -1, kind, 0, last)]
        return [(other, -1 if off > 0 else 1, kind, 0, abs(off) - 1)]

    def send(axis, kind, off, hops):
        mirrored = off if abs(off) == HOPS["x" if axis == "z" else "z"] else -off
        pair = [(axis, 1, kind, off, hops), (axis, -1, kind, mirrored, hops)]
        for message in pair:
            await_messages(brought(message))
            ring(message, hops).start()
            sent.append(message)

    def brings(message, dz):
        axis, sign, _, off, hops = message
        if axis == "x":
            return off == dz
        return dz == HOPS["z"] if hops == HOPS["z"] - 1 else dz == -sign * (hops + 1)

    def act(i, owner, first, size, to, src=None):
        there = A.at[part(owner * shard + first, hs, size)]
        return pltpu.make_async_remote_copy(
            src_ref=there if src is None else src, dst_ref=there,
            send_sem=act_send.at[i], recv_sem=act_recv.at[i],
            device_id=(row, to), device_id_type=MESH)

    low, high = acts.at[pl.ds(0, hs)], acts.at[pl.ds(hs, hs)]
    act_out = {
        0: act(0, col, 0, hs, up, low), 3: act(3, col, hs, hs, down, high),
        1: act(1, col, hs, hs, up, high), 4: act(4, col, 0, hs, down, low),
        6: act(6, col, 0, shard, twin, acts),
        2: act(2, down, 0, hs, up), 5: act(5, up, hs, hs, down),
        7: act(7, down, 0, shard, twin), 8: act(8, up, 0, shard, twin),
        9: act(9, far, 0, hs, twin), 10: act(10, far, hs, hs, twin),
    }
    swap = 1 - 2 * core
    act_in = {
        0: act(0, down, 0, hs, up), 1: act(1, down, hs, hs, up), 2: act(2, far, 0, hs, up),
        3: act(3, up, hs, hs, down), 4: act(4, up, 0, hs, down), 5: act(5, far, hs, hs, down),
        6: act(6, twin, 0, shard, twin), 7: act(7, down + swap, 0, shard, twin),
        8: act(8, up + swap, 0, shard, twin), 9: act(9, far + swap, 0, hs, twin),
        10: act(10, far + swap, hs, hs, twin),
    }
    act_steps = {
        "own low": ((), (0, 3, 6)), "own high": ((), (1, 4)), "near": ((0, 3), (2, 5)),
        "cross": ((1, 4), (7, 8)), "far": ((2, 5), (9, 10)), "all": ((6, 7, 8, 9, 10), ()),
    }

    def add_products(dzs):
        for dz in dzs:
            await_messages([m for m in sent if brings(m, dz)])

        def add(i, carry):
            dz = dzs[0] if len(dzs) == 1 else dzs[0] + i
            if len(dzs) == 2:
                dz = dzs[0] + i * (Z + dzs[1] - dzs[0])
            if len(dzs) == 3:
                dz = i + (Z - 3) * div(i, 2)
            tokens = part(rem(z + dz, Z) * (X * tb), X * tb, X * tb)
            G[...] += lax.dot_general(
                A[tokens, :], B[tokens, :], (((0,), (0,)), ((), ())), preferred_element_type=F32)
            return carry

        if len(dzs) == 1:
            add(0, 0)
        else:
            lax.fori_loop(0, len(dzs), add, 0)

    for entry in ORDER:
        if isinstance(entry, str):
            arrive, leave = act_steps[entry]
            for i in arrive:
                act_in[i].wait_recv()
            for i in leave:
                act_out[i].start()
            if entry == "own high":
                loads[0].wait()
                loads[1].wait()
                G[...] = jnp.zeros_like(G)
        elif entry[0] in ("x", "z"):
            send(*entry)
        else:
            add_products(entry)
    for load in loads[2:]:
        load.wait()

    def exchange(phase, src, got, axis, send_sem, recv_sem):
        me, size = (row, R) if axis == "row" else (col, C)
        steps = sorted(range(1, size), key=lambda i: -hops_to(axis, i))

        def copy(i, slot):
            to = rem(me + i, size)
            return pltpu.make_async_remote_copy(
                src_ref=src, dst_ref=got.at[phase, slot],
                send_sem=send_sem.at[phase, i], recv_sem=recv_sem.at[phase, i],
                device_id=(to, col) if axis == "row" else (row, to), device_id_type=MESH)

        def start():
            for i in steps:
                copy(i, me).start()
            got[phase, me] = src[...]

        def result():
            for i in reversed(steps):
                copy(i, rem(me + size - i, size)).wait_recv()
            return jnp.sum(got[phase, pl.ds(0, size)], axis=0)

        def drain():
            for i in steps:
                copy(i, me).wait_send()

        return start, result, drain

    def hops_to(axis, i):
        if axis == "row":
            dz, dx = i // X, i % X
            return min(dz, Z - dz) + min(dx, X - dx)
        return min(i // 2, Y - i // 2) + i % 2

    def whole(tile):
        return jnp.sum(tile, axis=(0, 1), keepdims=True)

    lane_ids = lax.broadcasted_iota(jnp.int32, (1, LANES), 1)

    def sums(phase, block):
        def rows_of(i, col_sum):
            at = part(i * LANES, LANES, LANES)
            row_sum = jnp.zeros((LANES, LANES), F32)
            col_sums = []
            for j in range(nc):
                square = block(i, at, j)
                row_sum += square
                col_sums.append(jnp.sum(square.reshape(LANES // 8, 8, LANES), axis=0))
            row_part[phase, pl.ds(i, 1), :] = jnp.sum(row_sum.T, axis=0, keepdims=True)
            return col_sum + jnp.concatenate(col_sums, 1)

        return lax.fori_loop(0, nr, rows_of, jnp.zeros((8, cols), F32))

    def reduced(phase, col_sum, beside, meanwhile):
        values = [whole(col_sum)] + beside
        packed_values = jnp.zeros((1, LANES), F32)
        for lane, value in enumerate(values):
            packed_values = jnp.where(lane_ids == lane, value, packed_values)
        tot_part[phase] = packed_values
        by_tot = exchange(phase, tot_part.at[phase], tot_got, "row", tot_send, tot_recv)
        by_tot[0]()
        col_sum = jnp.sum(col_sum, axis=0, keepdims=True)
        for j in range(nc):
            col_part[phase, j:j + 1, :] = col_sum[:, j * LANES:(j + 1) * LANES]
        by_col = exchange(phase, col_part.at[phase], col_got, "row", col_send, col_recv)
        by_row = exchange(phase, row_part.at[phase], row_got, "col", row_send, row_recv)
        by_col[0]()
        by_row[0]()
        meanwhile()
        tot_rows = by_tot[1]()
        tot_part[2 + phase] = tot_rows
        by_all = exchange(2 + phase, tot_part.at[2 + phase], tot_got, "col", tot_send, tot_recv)
        by_all[0]()
        col_all = by_col[1]()
        row_all = by_row[1]()
        for one in (by_tot, by_col, by_row):
            one[2]()
        tot_all = by_all[1]()

        def drain():
            by_all[2]()
        return row_all, col_all, tot_all, tot_rows, drain

    def down_rows(factor_ref, i):
        return jnp.broadcast_to(factor_ref[pl.ds(i, 1), :], (LANES, LANES)).T

    col_part[...] = jnp.zeros_like(col_part)
    row_part[...] = jnp.zeros_like(row_part)

    def squared(i, at, j):
        g = G[at, j * LANES:(j + 1) * LANES]
        return g * g

    def gather_drain():
        for message in sent:
            ring(message, message[4]).wait_send()
        for copy in act_out.values():
            copy.wait_send()

    col_sum = sums(0, squared)
    row_all, col_all, tot_all, tot_rows, drain0 = reduced(
        0, col_sum, [whole(states[0]), whole(states[2])], gather_drain)
    total, row_state_sum, row_conf_sum = tot_all[:, 0:1], tot_rows[:, 1:2], tot_rows[:, 2:3]
    scaling = jnp.minimum(1.0, (full_rows * full_cols) ** 0.5 / jnp.sqrt(total + 1e-06))
    keep, fresh = second_decay, 1.0 - second_decay
    spread = scaling * scaling
    row_new = keep * states[0] + fresh * (spread * row_all * (1.0 / full_cols) + tiny_moment)
    col_new = keep * states[1] + fresh * (spread * col_all * (1.0 / full_rows) + tiny_moment)
    row_mean = keep * (row_state_sum * (1.0 / full_rows)) + fresh * (
        spread * total * (1.0 / (full_rows * full_cols)) + tiny_moment)
    packed[0] = row_new
    packed[1] = col_new
    row_part[2] = lax.rsqrt(row_new)
    col_scale = lax.rsqrt(col_new) * (scaling * jnp.sqrt(row_mean))

    def strays(i, at, j):
        here = (at, slice(j * LANES, (j + 1) * LANES))
        direction = G[here] * down_rows(row_part.at[2], i) * col_scale[j:j + 1, :]
        stray = direction - M[here]
        M[here] = M[here] + (1.0 - first_decay) * stray
        return stray * stray

    col_sum = sums(1, strays)
    row_all, col_all, tot_all, _, drain1 = reduced(1, col_sum, [], drain0)
    total = tot_all[:, 0:1]
    share = first_decay * first_decay
    row_conf_new = keep * states[2] + fresh * (row_all * (share / full_cols) + tiny_confidence)
    col_conf_new = keep * states[3] + fresh * (col_all * (share / full_rows) + tiny_confidence)
    conf_mean = keep * (row_conf_sum * (1.0 / full_rows)) + fresh * (
        total * (share / (full_rows * full_cols)) + tiny_confidence)
    packed[2] = row_conf_new
    packed[3] = col_conf_new
    packed[4] = lax.rsqrt(row_conf_new)
    packed[5] = lax.rsqrt(col_conf_new) * jnp.sqrt(conf_mean)
    drain1()


def finish(M, packed, moment_out, update_out, row_out, col_out, row_conf_out, col_conf_out, U, sem, block_sem):
    rows, cols = U.shape
    nr, nc = rows // LANES, cols // LANES
    stores = [pltpu.make_async_copy(M, moment_out, sem.at[0])]
    for k, (out, n) in enumerate(((row_out, nr), (col_out, nc), (row_conf_out, nr), (col_conf_out, nc))):
        stores.append(pltpu.make_async_copy(packed.at[k, pl.ds(0, n)], out, sem.at[1 + k]))
    for store in stores:
        store.start()

    def block_store(i):
        at = pl.ds(pl.multiple_of(i * LANES, LANES), LANES)
        return pltpu.make_async_copy(U.at[at], update_out.at[at], block_sem.at[i])

    def scale_block(i, carry):
        at = pl.ds(pl.multiple_of(i * LANES, LANES), LANES)
        scale = jnp.broadcast_to(packed[4, pl.ds(i, 1), :], (LANES, LANES)).T
        for j in range(nc):
            here = (at, slice(j * LANES, (j + 1) * LANES))
            U[here] = M[here] * scale * packed[5, j:j + 1, :]
        block_store(i).start()
        return carry

    def wait_block(i, carry):
        block_store(i).wait()
        return carry

    lax.fori_loop(0, nr, scale_block, 0)
    lax.fori_loop(0, nr, wait_block, 0)
    for store in stores:
        store.wait()


def on_device(acts, out_grads, moment, row_state, col_state, row_conf, col_conf):
    R, C = lax.axis_size("row"), lax.axis_size("col")
    rows, cols = moment.shape
    nr, nc = rows // LANES, cols // LANES
    dma = pltpu.SemaphoreType.DMA
    big = jax.ShapeDtypeStruct((rows, cols), F32)
    by_row, by_col = (jax.ShapeDtypeStruct((n, LANES), F32) for n in (nr, nc))
    in_hbm = pl.BlockSpec(memory_space=pltpu.HBM)
    in_vmem = pl.BlockSpec(memory_space=pltpu.VMEM)
    tokens = R * out_grads.shape[0]
    moment_new, packed = pl.pallas_call(
        functools.partial(kernel, R, C),
        out_shape=(pltpu.VMEM((rows, cols), F32), pltpu.VMEM((6, 8, LANES), F32)),
        in_specs=[in_hbm] * 7,
        out_specs=(in_vmem,) * 2,
        scratch_shapes=[
            pltpu.VMEM((tokens, rows), acts.dtype),
            pltpu.VMEM((tokens, cols), out_grads.dtype),
            pltpu.VMEM((rows, cols), F32),
            pltpu.VMEM((4, 8, LANES), F32),
            pltpu.VMEM((3, 8, LANES), F32),
            pltpu.VMEM((2, C, 8, LANES), F32),
            pltpu.VMEM((2, 8, LANES), F32),
            pltpu.VMEM((2, R, 8, LANES), F32),
            pltpu.VMEM((4, 1, LANES), F32),
            pltpu.VMEM((4, R, 1, LANES), F32),
            dma((4, 20)), dma((4, 20)), dma((11,)), dma((11,)), dma((7,)),
            dma((2, C)), dma((2, C)), dma((2, R)), dma((2, R)), dma((4, R)), dma((4, R)),
        ],
        compiler_params=pltpu.CompilerParams(
            collective_id=0, has_side_effects=True, vmem_limit_bytes=40 * 2**20),
        cost_estimate=pl.CostEstimate(
            flops=2 * tokens * rows * cols, transcendentals=0, bytes_accessed=30 * 2**20),
        name="came_step",
    )(*(pltpu.with_memory_space_constraint(v, pltpu.HBM) for v in (
        acts, out_grads, moment, row_state.reshape(nr, LANES), col_state.reshape(nc, LANES),
        row_conf.reshape(nr, LANES), col_conf.reshape(nc, LANES))))
    outs = pl.pallas_call(
        finish,
        out_shape=(big, big, by_row, by_col, by_row, by_col),
        in_specs=[in_vmem] * 2,
        out_specs=(in_hbm,) * 6,
        scratch_shapes=[pltpu.VMEM((rows, cols), F32), dma((5,)), dma((nr,))],
        compiler_params=pltpu.CompilerParams(vmem_limit_bytes=16 * 2**20),
        cost_estimate=pl.CostEstimate(
            flops=2 * rows * cols, transcendentals=0, bytes_accessed=12 * rows * cols),
        name="finish",
    )(moment_new, packed)
    return outs[0], outs[1], *(out.reshape(-1) for out in outs[2:])


def solution(mesh):
    placed = (
        P("col", "row"),
        P("row", "col"),
        P("row", "col"),
        P("row"),
        P("col"),
        P("row"),
        P("col"),
    )
    return jax.shard_map(
        on_device,
        mesh=mesh,
        in_specs=placed,
        out_specs=(P("row", "col"), P("row", "col"), P("row"), P("col"), P("row"), P("col")),
        check_vma=False,
    )
```

time: 123 us -> 90 us (0.73)
  Pallas kernels: 110 us -> 89.3 us
  local copies, waits for them, and re-layouts: 12.4 us -> 0 us
    pallas_call x1 -> x2, Pallas kernels: 110 us -> 89.3 us  [the longest x1 86.2 us: on_device(): pl.pallas_call(functools.partial(kernel, R, C), out_shape=(pltpu.VMEM((ro...]
    unnamed x20 -> x0, local copies, waits for them, and re-layouts: 12.4 us -> none
where the time goes in v2:
time: 90 us; the launch traced here: 89.9 us
  Pallas kernels  89.3 us (99%)
    pallas_call x1, Pallas kernels, on_device(): pl.pallas_call(functools.partial(kernel, R, C), out_shape=(pltpu.VMEM((ro...  86.2 us
    pallas_call x1, Pallas kernels, on_device(): pl.pallas_call(finish, out_shape=(big, big, by_row, by_col, by_row, by_co...  3.09 us

profile of v2, /device:TPU:1, one launch (start us, length us, event | category | flops | bytes accessed | tf_op | source)
XLA Modules:
  0.0 89.9 jit_solution(7579586923728811087)
XLA Ops:
  0.6 86.2 %came_step.1 = (f32[896,1024]{1,0:T(8,128)S(1)}, f32[6,8,128]{2,1,0:T(8,128)S(1)}) custom-call(bf16[512,896]{1,0:T(8,128)(2,1)} %acts.1, bf16[128,1024]{1,0:T(8,128)(2,1)} %grads.1, f32[896,1024]{1,0:T(8,128)} %moment.1, f32[7,128]{1,0:T(8,128)} %bitcast.8, f32[8,128]{1,0:T(8,128)} %bitcast.9, f32[7,128]{1,0:T(8,128)} %bitcast.10, f32[8,128]{1,0:T(8,128)} %bitcast.11), custom_call_target="tpu_custom_call" | custom-call | flops 7516192768 | bytes 31457280 | tf_op jit(solution)/shard_map/came_step/pallas_call | solution.py:390
  86.8 3.1 %finish.1 = (f32[896,1024]{1,0:T(8,128)}, f32[896,1024]{1,0:T(8,128)}, f32[7,128]{1,0:T(8,128)}, f32[8,128]{1,0:T(8,128)}, f32[7,128]{1,0:T(8,128)}, /*index=5*/f32[8,128]{1,0:T(8,128)}) custom-call(f32[896,1024]{1,0:T(8,128)S(1)} %get-tuple-element.14.M, f32[6,8,128]{2,1,0:T(8,128)S(1)} %get-tuple-element.15.packed), custom_call_target="tpu_custom_call" | custom-call | flops 1835008 | bytes 11010048 | tf_op jit(solution)/shard_map/finish/pallas_call | solution.py:417

commit v3 on v2

--- a/solution.py
+++ b/solution.py
@@ -22,7 +22,7 @@
 ORDER = (
     ("z", "Q", 0, 0), ("x", "P", 0, 0), ("x", "Q", 0, 0), ("z", "P", 0, 0), "own low",
     ("z", "P", 1, 0), ("x", "P", 0, 1), ("x", "Q", 1, 0), ("z", "Q", 0, 1), "own high",
-    ("x", "Q", -1, 0), ("z", "P", -1, 0), ("z", "P", 2, 0), ("x", "Q", 0, 1),
+    ("x", "Q", -1, 0), ("z", "P", -1, 0), "strip", ("z", "P", 2, 0), ("x", "Q", 0, 1),
     ("z", "Q", 0, 2), ("x", "Q", 2, 0), ("z", "P", 0, 1), ("x", "Q", 1, 1), "near",
     ("z", "P", 1, 1), ("x", "Q", -2, 0), ("x", "Q", -1, 1), ("z", "Q", 0, 3), ("z", "P", -1, 1),
     ("x", "Q", 3, 0), ("z", "P", 2, 1), "cross",
@@ -30,15 +30,16 @@
     ("x", "Q", -2, 1), ("z", "P", 2, 2), ("x", "Q", 4, 0), "far",
     ("z", "P", 0, 3), ("z", "P", 1, 3), "all", (0, 1, -1),
     ("x", "Q", 3, 1), ("z", "P", -1, 3), ("x", "Q", -3, 1), ("z", "P", 2, 3), (2, -2),
-    ("x", "Q", 4, 1), (3, -3), (4,),
+    ("x", "Q", 4, 1), ((3, 0), (3, 1), (3, -1), (-3, 0), (-3, 1), (-3, -1)),
+    ((4, 0), (4, 1), (4, -1), (3, 2)), ((-3, 2), (4, 2)),
 )
 HOPS = {"z": 4, "x": 2}
 
 
 def kernel(R, C, acts, grads, moment, row_state, col_state, row_conf, col_conf, M, packed,
-           A, B, G, states, row_part, row_got, col_part, col_got, tot_part, tot_got,
+           A, B, G, states, row_part, row_got, col_part, col_got, tot_part, tot_got, all_part, all_got,
            ring_send, ring_recv, act_send, act_recv, load_sem,
-           row_send, row_recv, col_send, col_recv, tot_send, tot_recv):
+           row_send, row_recv, col_send, col_recv, tot_send, tot_recv, all_send, all_recv):
     Z, Y = R // X, C // 2
     row, col = lax.axis_index("row"), lax.axis_index("col")
     div, rem = lax.div, lax.rem
@@ -53,6 +54,9 @@
     def at_offset(dz, dx):
         return rem(z + dz + Z, Z) * X + rem(x + dx + X, X)
 
+    across = at_offset(0, 2)
+
+
     def part(first, unit, size):
         return pl.ds(pl.multiple_of(first, unit), size)
 
@@ -61,7 +65,7 @@
     far, twin = rem(y + 2, Y) * 2 + core, y * 2 + 1 - core
 
     barrier = pltpu.get_barrier_semaphore()
-    for r in ring_to.values():
+    for r in (*ring_to.values(), across):
         pl.semaphore_signal(barrier, inc=1, device_id=(r, col), device_id_type=MESH)
     for c in (up, down, twin):
         pl.semaphore_signal(barrier, inc=1, device_id=(row, c), device_id_type=MESH)
@@ -78,11 +82,15 @@
     states[...] = jnp.zeros_like(states)
     for load in loads:
         load.start()
-    pl.semaphore_wait(barrier, 7)
+    pl.semaphore_wait(barrier, 8)
 
     def extent(message):
         axis, sign, kind, off, hops = message
         first, size = (0, p_rows) if kind == "P" else (p_rows, tb - p_rows)
+        if axis == "z" and kind == "P" and off == HOPS["x"]:
+            size += 16
+        if axis == "x" and kind == "Q" and hops == HOPS["x"] - 1:
+            first, size = first + 16, size - 16
         if hops == HOPS[axis] - 1:
             low = (size // 2 + 15) // 16 * 16
             low = size - low if off % 2 else low
@@ -107,6 +115,12 @@
             src_ref=grads.at[pl.ds(first, size)] if made == 0 and off == 0 else there, dst_ref=there,
             send_sem=ring_send.at[lane, number], recv_sem=ring_recv.at[lane, number],
             device_id=(ring_to[axis, sign], col), device_id_type=MESH)
+
+    def strip(owner):
+        return pltpu.make_async_remote_copy(
+            src_ref=grads.at[pl.ds(p_rows, 16)], dst_ref=B.at[part(owner * tb + p_rows, 16, 16)],
+            send_sem=act_send.at[11], recv_sem=act_recv.at[11],
+            device_id=(across, col), device_id_type=MESH)
 
     sent, landed = [], set()
 
@@ -169,27 +183,31 @@
     act_steps = {
         "own low": ((), (0, 3, 6)), "own high": ((), (1, 4)), "near": ((0, 3), (2, 5)),
         "cross": ((1, 4), (7, 8)), "far": ((2, 5), (9, 10)), "all": ((6, 7, 8, 9, 10), ()),
+        "strip": ((), ()),
     }
 
-    def add_products(dzs):
+    def accumulate(a, b):
+        G[...] += lax.dot_general(a, b, (((0,), (0,)), ((), ())), preferred_element_type=F32)
+
+    def add_planes(dzs):
         for dz in dzs:
             await_messages([m for m in sent if brings(m, dz)])
 
         def add(i, carry):
-            dz = dzs[0] if len(dzs) == 1 else dzs[0] + i
-            if len(dzs) == 2:
-                dz = dzs[0] + i * (Z + dzs[1] - dzs[0])
-            if len(dzs) == 3:
-                dz = i + (Z - 3) * div(i, 2)
+            dz = i + (Z - 3) * div(i, 2) if len(dzs) == 3 else dzs[0] + i * (Z + dzs[1] - dzs[0])
             tokens = part(rem(z + dz, Z) * (X * tb), X * tb, X * tb)
-            G[...] += lax.dot_general(
-                A[tokens, :], B[tokens, :], (((0,), (0,)), ((), ())), preferred_element_type=F32)
+            accumulate(A[tokens, :], B[tokens, :])
             return carry
 
-        if len(dzs) == 1:
-            add(0, 0)
-        else:
-            lax.fori_loop(0, len(dzs), add, 0)
+        lax.fori_loop(0, len(dzs), add, 0)
+
+    def add_blocks(offsets):
+        for dz, dx in offsets:
+            await_messages([m for m in sent if brings(m, dz) and (
+                m[3] == dx if m[0] == "z" else dx == -m[1] * (m[4] + 1) or (dx == 2 and m[4] == 1))])
+        tokens = [part(at_offset(dz, dx) * tb, tb, tb) for dz, dx in offsets]
+        accumulate(jnp.concatenate([A[t, :] for t in tokens], 0),
+                   jnp.concatenate([B[t, :] for t in tokens], 0))
 
     for entry in ORDER:
         if isinstance(entry, str):
@@ -198,14 +216,20 @@
                 act_in[i].wait_recv()
             for i in leave:
                 act_out[i].start()
+            if entry == "own low":
+                strip(row).start()
+            if entry == "strip":
+                strip(across).wait_recv()
             if entry == "own high":
                 loads[0].wait()
                 loads[1].wait()
                 G[...] = jnp.zeros_like(G)
         elif entry[0] in ("x", "z"):
             send(*entry)
+        elif isinstance(entry[0], int):
+            add_planes(entry)
         else:
-            add_products(entry)
+            add_blocks(entry)
     for load in loads[2:]:
         load.wait()
 
@@ -213,26 +237,26 @@
         me, size = (row, R) if axis == "row" else (col, C)
         steps = sorted(range(1, size), key=lambda i: -hops_to(axis, i))
 
-        def copy(i, slot):
+        def copy(i, source, target):
             to = rem(me + i, size)
             return pltpu.make_async_remote_copy(
-                src_ref=src, dst_ref=got.at[phase, slot],
-                send_sem=send_sem.at[phase, i], recv_sem=recv_sem.at[phase, i],
+                src_ref=source, dst_ref=target,
+                send_sem=send_sem.at[phase], recv_sem=recv_sem.at[phase],
                 device_id=(to, col) if axis == "row" else (row, to), device_id_type=MESH)
+
+        others = got.at[phase, pl.ds(0, size - 1)]
 
         def start():
             for i in steps:
-                copy(i, me).start()
+                copy(i, src, got.at[phase, me]).start()
             got[phase, me] = src[...]
 
         def result():
-            for i in reversed(steps):
-                copy(i, rem(me + size - i, size)).wait_recv()
+            copy(1, others, others).wait_recv()
             return jnp.sum(got[phase, pl.ds(0, size)], axis=0)
 
         def drain():
-            for i in steps:
-                copy(i, me).wait_send()
+            copy(1, others, others).wait_send()
 
         return start, result, drain
 
@@ -245,15 +269,14 @@
     def whole(tile):
         return jnp.sum(tile, axis=(0, 1), keepdims=True)
 
-    lane_ids = lax.broadcasted_iota(jnp.int32, (1, LANES), 1)
-
     def sums(phase, block):
         def rows_of(i, col_sum):
             at = part(i * LANES, LANES, LANES)
             row_sum = jnp.zeros((LANES, LANES), F32)
             col_sums = []
+            scale = down_rows(row_part.at[2], i) if phase else None
             for j in range(nc):
-                square = block(i, at, j)
+                square = block(at, j, scale)
                 row_sum += square
                 col_sums.append(jnp.sum(square.reshape(LANES // 8, 8, LANES), axis=0))
             row_part[phase, pl.ds(i, 1), :] = jnp.sum(row_sum.T, axis=0, keepdims=True)
@@ -262,34 +285,31 @@
         return lax.fori_loop(0, nr, rows_of, jnp.zeros((8, cols), F32))
 
     def reduced(phase, col_sum, beside, meanwhile):
-        values = [whole(col_sum)] + beside
-        packed_values = jnp.zeros((1, LANES), F32)
-        for lane, value in enumerate(values):
-            packed_values = jnp.where(lane_ids == lane, value, packed_values)
-        tot_part[phase] = packed_values
+        col_sum = jnp.sum(col_sum, axis=0, keepdims=True)
+        col_sums = [col_sum[:, j * LANES:(j + 1) * LANES] for j in range(nc)]
+        tot_part[phase] = jnp.concatenate([functools.reduce(jnp.add, col_sums)] + beside, 1)
         by_tot = exchange(phase, tot_part.at[phase], tot_got, "row", tot_send, tot_recv)
         by_tot[0]()
-        col_sum = jnp.sum(col_sum, axis=0, keepdims=True)
         for j in range(nc):
-            col_part[phase, j:j + 1, :] = col_sum[:, j * LANES:(j + 1) * LANES]
+            col_part[phase, j:j + 1, :] = col_sums[j]
         by_col = exchange(phase, col_part.at[phase], col_got, "row", col_send, col_recv)
         by_row = exchange(phase, row_part.at[phase], row_got, "col", row_send, row_recv)
         by_col[0]()
         by_row[0]()
         meanwhile()
         tot_rows = by_tot[1]()
-        tot_part[2 + phase] = tot_rows
-        by_all = exchange(2 + phase, tot_part.at[2 + phase], tot_got, "col", tot_send, tot_recv)
+        all_part[phase] = tot_rows[:, :LANES]
+        by_all = exchange(phase, all_part.at[phase], all_got, "col", all_send, all_recv)
         by_all[0]()
         col_all = by_col[1]()
         row_all = by_row[1]()
         for one in (by_tot, by_col, by_row):
             one[2]()
-        tot_all = by_all[1]()
+        total = whole(by_all[1]())
 
         def drain():
             by_all[2]()
-        return row_all, col_all, tot_all, tot_rows, drain
+        return row_all, col_all, total, tot_rows, drain
 
     def down_rows(factor_ref, i):
         return jnp.broadcast_to(factor_ref[pl.ds(i, 1), :], (LANES, LANES)).T
@@ -297,7 +317,7 @@
     col_part[...] = jnp.zeros_like(col_part)
     row_part[...] = jnp.zeros_like(row_part)
 
-    def squared(i, at, j):
+    def squared(at, j, scale):
         g = G[at, j * LANES:(j + 1) * LANES]
         return g * g
 
@@ -306,14 +326,14 @@
             ring(message, message[4]).wait_send()
         for copy in act_out.values():
             copy.wait_send()
+        strip(row).wait_send()
 
     col_sum = sums(0, squared)
-    row_all, col_all, tot_all, tot_rows, drain0 = reduced(
-        0, col_sum, [whole(states[0]), whole(states[2])], gather_drain)
-    total, row_state_sum, row_conf_sum = tot_all[:, 0:1], tot_rows[:, 1:2], tot_rows[:, 2:3]
-    scaling = jnp.minimum(1.0, (full_rows * full_cols) ** 0.5 / jnp.sqrt(total + 1e-06))
+    states_sums = [jnp.sum(states[k], axis=0, keepdims=True) for k in (0, 2)]
+    row_all, col_all, total, tot_rows, drain0 = reduced(0, col_sum, states_sums, gather_drain)
+    row_state_sum, row_conf_sum = whole(tot_rows[:, LANES:2 * LANES]), whole(tot_rows[:, 2 * LANES:])
+    spread = jnp.minimum(1.0, (full_rows * full_cols) / (total + 1e-06))
     keep, fresh = second_decay, 1.0 - second_decay
-    spread = scaling * scaling
     row_new = keep * states[0] + fresh * (spread * row_all * (1.0 / full_cols) + tiny_moment)
     col_new = keep * states[1] + fresh * (spread * col_all * (1.0 / full_rows) + tiny_moment)
     row_mean = keep * (row_state_sum * (1.0 / full_rows)) + fresh * (
@@ -321,18 +341,17 @@
     packed[0] = row_new
     packed[1] = col_new
     row_part[2] = lax.rsqrt(row_new)
-    col_scale = lax.rsqrt(col_new) * (scaling * jnp.sqrt(row_mean))
-
-    def strays(i, at, j):
+    col_scale = lax.rsqrt(col_new) * jnp.sqrt(spread * row_mean)
+
+    def strays(at, j, scale):
         here = (at, slice(j * LANES, (j + 1) * LANES))
-        direction = G[here] * down_rows(row_part.at[2], i) * col_scale[j:j + 1, :]
+        direction = G[here] * scale * col_scale[j:j + 1, :]
         stray = direction - M[here]
         M[here] = M[here] + (1.0 - first_decay) * stray
         return stray * stray
 
     col_sum = sums(1, strays)
-    row_all, col_all, tot_all, _, drain1 = reduced(1, col_sum, [], drain0)
-    total = tot_all[:, 0:1]
+    row_all, col_all, total, _, drain1 = reduced(1, col_sum, [jnp.zeros((1, 2 * LANES), F32)], drain0)
     share = first_decay * first_decay
     row_conf_new = keep * states[2] + fresh * (row_all * (share / full_cols) + tiny_confidence)
     col_conf_new = keep * states[3] + fresh * (col_all * (share / full_rows) + tiny_confidence)
@@ -401,10 +420,12 @@
             pltpu.VMEM((2, C, 8, LANES), F32),
             pltpu.VMEM((2, 8, LANES), F32),
             pltpu.VMEM((2, R, 8, LANES), F32),
-            pltpu.VMEM((4, 1, LANES), F32),
-            pltpu.VMEM((4, R, 1, LANES), F32),
-            dma((4, 20)), dma((4, 20)), dma((11,)), dma((11,)), dma((7,)),
-            dma((2, C)), dma((2, C)), dma((2, R)), dma((2, R)), dma((4, R)), dma((4, R)),
+            pltpu.VMEM((2, 1, 3 * LANES), F32),
+            pltpu.VMEM((2, R, 1, 3 * LANES), F32),
+            pltpu.VMEM((2, 1, LANES), F32),
+            pltpu.VMEM((2, C, 1, LANES), F32),
+            dma((4, 20)), dma((4, 20)), dma((12,)), dma((12,)), dma((7,)),
+            dma((2,)), dma((2,)), dma((2,)), dma((2,)), dma((2,)), dma((2,)), dma((2,)), dma((2,)),
         ],
         compiler_params=pltpu.CompilerParams(
             collective_id=0, has_side_effects=True, vmem_limit_bytes=40 * 2**20),

time: 90 us -> 86.8 us (0.964)
  Pallas kernels: 89.3 us -> 86.1 us
    pallas_call x1, Pallas kernels: 86.2 us -> 83 us  [on_device(): pl.pallas_call(functools.partial(kernel, R, C), out_shape=(pltpu.VMEM((ro...]
where the time goes in v3:
time: 86.8 us; the launch traced here: 86.7 us
  Pallas kernels  86.1 us (99%)
    pallas_call x1, Pallas kernels, on_device(): pl.pallas_call(functools.partial(kernel, R, C), out_shape=(pltpu.VMEM((ro...  83 us
    pallas_call x1, Pallas kernels, on_device(): pl.pallas_call(finish, out_shape=(big, big, by_row, by_col, by_row, by_co...  3.09 us

profile of v3, /device:TPU:1, one launch (start us, length us, event | category | flops | bytes accessed | tf_op | source)
XLA Modules:
  0.0 86.7 jit_solution(15262190231382142126)
XLA Ops:
  0.6 83.0 %came_step.1 = (f32[896,1024]{1,0:T(8,128)S(1)}, f32[6,8,128]{2,1,0:T(8,128)S(1)}) custom-call(bf16[512,896]{1,0:T(8,128)(2,1)} %acts.1, bf16[128,1024]{1,0:T(8,128)(2,1)} %grads.1, f32[896,1024]{1,0:T(8,128)} %moment.1, f32[7,128]{1,0:T(8,128)} %bitcast.8, f32[8,128]{1,0:T(8,128)} %bitcast.9, f32[7,128]{1,0:T(8,128)} %bitcast.10, f32[8,128]{1,0:T(8,128)} %bitcast.11), custom_call_target="tpu_custom_call" | custom-call | flops 7516192768 | bytes 31457280 | tf_op jit(solution)/shard_map/came_step/pallas_call | solution.py:409
  83.6 3.1 %finish.1 = (f32[896,1024]{1,0:T(8,128)}, f32[896,1024]{1,0:T(8,128)}, f32[7,128]{1,0:T(8,128)}, f32[8,128]{1,0:T(8,128)}, f32[7,128]{1,0:T(8,128)}, /*index=5*/f32[8,128]{1,0:T(8,128)}) custom-call(f32[896,1024]{1,0:T(8,128)S(1)} %get-tuple-element.14.M, f32[6,8,128]{2,1,0:T(8,128)S(1)} %get-tuple-element.15.packed), custom_call_target="tpu_custom_call" | custom-call | flops 1835008 | bytes 11010048 | tf_op jit(solution)/shard_map/finish/pallas_call | solution.py:438

commit v4 on v3

--- a/solution.py
+++ b/solution.py
@@ -26,18 +26,16 @@
     ("z", "Q", 0, 2), ("x", "Q", 2, 0), ("z", "P", 0, 1), ("x", "Q", 1, 1), "near",
     ("z", "P", 1, 1), ("x", "Q", -2, 0), ("x", "Q", -1, 1), ("z", "Q", 0, 3), ("z", "P", -1, 1),
     ("x", "Q", 3, 0), ("z", "P", 2, 1), "cross",
-    ("x", "Q", 2, 1), ("z", "P", 0, 2), ("x", "Q", -3, 0), ("z", "P", 1, 2), ("z", "P", -1, 2),
-    ("x", "Q", -2, 1), ("z", "P", 2, 2), ("x", "Q", 4, 0), "far",
-    ("z", "P", 0, 3), ("z", "P", 1, 3), "all", (0, 1, -1),
-    ("x", "Q", 3, 1), ("z", "P", -1, 3), ("x", "Q", -3, 1), ("z", "P", 2, 3), (2, -2),
-    ("x", "Q", 4, 1), ((3, 0), (3, 1), (3, -1), (-3, 0), (-3, 1), (-3, -1)),
-    ((4, 0), (4, 1), (4, -1), (3, 2)), ((-3, 2), (4, 2)),
+    ("x", "Q", 2, 1), ("x", "Q", -3, 0), ("z", "P", 0, 2), ("z", "P", 1, 2), ("x", "Q", -2, 1),
+    ("z", "P", -1, 2), ("x", "Q", 4, 0), ("z", "P", 2, 2), "far", ("x", "Q", 3, 1), ("z", "P", 0, 3), "all",
 )
+FOURS_ORDER = ((), (("x", "Q", -3, 1),), (("z", "P", 1, 3),), (("z", "P", -1, 3),), (), (("x", "Q", 4, 1),))
+TWOS_ORDER = ((("z", "P", 2, 3),), (), (), ())
 HOPS = {"z": 4, "x": 2}
 
 
 def kernel(R, C, acts, grads, moment, row_state, col_state, row_conf, col_conf, M, packed,
-           A, B, G, states, row_part, row_got, col_part, col_got, tot_part, tot_got, all_part, all_got,
+           A, B, G, states, row_sums, row_scale, row_part, row_got, col_part, col_got, tot_part, tot_got, all_part, all_got,
            ring_send, ring_recv, act_send, act_recv, load_sem,
            row_send, row_recv, col_send, col_recv, tot_send, tot_recv, all_send, all_recv):
     Z, Y = R // X, C // 2
@@ -186,28 +184,41 @@
         "strip": ((), ()),
     }
 
-    def accumulate(a, b):
-        G[...] += lax.dot_general(a, b, (((0,), (0,)), ((), ())), preferred_element_type=F32)
-
-    def add_planes(dzs):
-        for dz in dzs:
-            await_messages([m for m in sent if brings(m, dz)])
-
-        def add(i, carry):
-            dz = i + (Z - 3) * div(i, 2) if len(dzs) == 3 else dzs[0] + i * (Z + dzs[1] - dzs[0])
-            tokens = part(rem(z + dz, Z) * (X * tb), X * tb, X * tb)
-            accumulate(A[tokens, :], B[tokens, :])
-            return carry
-
-        lax.fori_loop(0, len(dzs), add, 0)
-
-    def add_blocks(offsets):
+    def fours(i):
+        dz, odd = div(i + 1, 2) * (2 * rem(i, 2) - 1), div(i, 5)
+        return (dz, 0), (dz, 1), (dz, 3), (dz - 6 * odd, 2 - 2 * odd)
+
+    def twos(i):
+        return (5 - 2 * rem(i, 2) + div(i, 3), 1 + div(i + 1, 2)), (5 - div(i + 2, 3), i - 1)
+
+    def await_blocks(offsets):
         for dz, dx in offsets:
+            dz, dx = (dz + Z // 2 - 1) % Z - Z // 2 + 1, (dx + 1) % X - 1
             await_messages([m for m in sent if brings(m, dz) and (
                 m[3] == dx if m[0] == "z" else dx == -m[1] * (m[4] + 1) or (dx == 2 and m[4] == 1))])
-        tokens = [part(at_offset(dz, dx) * tb, tb, tb) for dz, dx in offsets]
-        accumulate(jnp.concatenate([A[t, :] for t in tokens], 0),
-                   jnp.concatenate([B[t, :] for t in tokens], 0))
+
+    def add_products(blocks, order):
+        def ahead(n):
+            for message in order[n]:
+                send(*message)
+            await_blocks(static_blocks(blocks, n))
+
+        def add(i, carry):
+            for n in range(len(order)):
+                pl.when(i == n)(functools.partial(ahead, n))
+            tokens = [part(at_offset(dz, dx) * tb, tb, tb) for dz, dx in blocks(i)]
+            G[...] += lax.dot_general(
+                jnp.concatenate([A[t, :] for t in tokens], 0), jnp.concatenate([B[t, :] for t in tokens], 0),
+                (((0,), (0,)), ((), ())), preferred_element_type=F32)
+            return carry
+
+        lax.fori_loop(0, len(order), add, 0)
+
+    def static_blocks(blocks, n):
+        if blocks is fours:
+            dz, odd = (n + 1) // 2 * (2 * (n % 2) - 1), n // 5
+            return (dz, 0), (dz, 1), (dz, 3), (dz - 6 * odd, 2 - 2 * odd)
+        return (5 - 2 * (n % 2) + n // 3, 1 + (n + 1) // 2), (5 - (n + 2) // 3, n - 1)
 
     for entry in ORDER:
         if isinstance(entry, str):
@@ -224,12 +235,10 @@
                 loads[0].wait()
                 loads[1].wait()
                 G[...] = jnp.zeros_like(G)
-        elif entry[0] in ("x", "z"):
+        else:
             send(*entry)
-        elif isinstance(entry[0], int):
-            add_planes(entry)
-        else:
-            add_blocks(entry)
+    add_products(fours, FOURS_ORDER)
+    add_products(twos, TWOS_ORDER)
     for load in loads[2:]:
         load.wait()
 
@@ -269,17 +278,16 @@
     def whole(tile):
         return jnp.sum(tile, axis=(0, 1), keepdims=True)
 
-    def sums(phase, block):
+    def sums(block):
         def rows_of(i, col_sum):
             at = part(i * LANES, LANES, LANES)
             row_sum = jnp.zeros((LANES, LANES), F32)
             col_sums = []
-            scale = down_rows(row_part.at[2], i) if phase else None
             for j in range(nc):
-                square = block(at, j, scale)
+                square = block(at, j)
                 row_sum += square
                 col_sums.append(jnp.sum(square.reshape(LANES // 8, 8, LANES), axis=0))
-            row_part[phase, pl.ds(i, 1), :] = jnp.sum(row_sum.T, axis=0, keepdims=True)
+            row_sums[at, :] = row_sum
             return col_sum + jnp.concatenate(col_sums, 1)
 
         return lax.fori_loop(0, nr, rows_of, jnp.zeros((8, cols), F32))
@@ -295,6 +303,9 @@
         by_col = exchange(phase, col_part.at[phase], col_got, "row", col_send, col_recv)
         by_row = exchange(phase, row_part.at[phase], row_got, "col", row_send, row_recv)
         by_col[0]()
+        for i in range(nr):
+            turned = row_sums[i * LANES:(i + 1) * LANES, :].T
+            row_part[phase, i:i + 1, :] = jnp.sum(turned, axis=0, keepdims=True)
         by_row[0]()
         meanwhile()
         tot_rows = by_tot[1]()
@@ -311,13 +322,14 @@
             by_all[2]()
         return row_all, col_all, total, tot_rows, drain
 
-    def down_rows(factor_ref, i):
-        return jnp.broadcast_to(factor_ref[pl.ds(i, 1), :], (LANES, LANES)).T
+    def down_rows(factors):
+        for i in range(nr):
+            row_scale[i * LANES:(i + 1) * LANES, :] = jnp.broadcast_to(factors[i:i + 1, :], (LANES, LANES)).T
 
     col_part[...] = jnp.zeros_like(col_part)
     row_part[...] = jnp.zeros_like(row_part)
 
-    def squared(at, j, scale):
+    def squared(at, j):
         g = G[at, j * LANES:(j + 1) * LANES]
         return g * g
 
@@ -328,7 +340,7 @@
             copy.wait_send()
         strip(row).wait_send()
 
-    col_sum = sums(0, squared)
+    col_sum = sums(squared)
     states_sums = [jnp.sum(states[k], axis=0, keepdims=True) for k in (0, 2)]
     row_all, col_all, total, tot_rows, drain0 = reduced(0, col_sum, states_sums, gather_drain)
     row_state_sum, row_conf_sum = whole(tot_rows[:, LANES:2 * LANES]), whole(tot_rows[:, 2 * LANES:])
@@ -338,19 +350,19 @@
     col_new = keep * states[1] + fresh * (spread * col_all * (1.0 / full_rows) + tiny_moment)
     row_mean = keep * (row_state_sum * (1.0 / full_rows)) + fresh * (
         spread * total * (1.0 / (full_rows * full_cols)) + tiny_moment)
+    down_rows(lax.rsqrt(row_new))
     packed[0] = row_new
     packed[1] = col_new
-    row_part[2] = lax.rsqrt(row_new)
     col_scale = lax.rsqrt(col_new) * jnp.sqrt(spread * row_mean)
 
-    def strays(at, j, scale):
+    def strays(at, j):
         here = (at, slice(j * LANES, (j + 1) * LANES))
-        direction = G[here] * scale * col_scale[j:j + 1, :]
+        direction = G[here] * row_scale[at, :] * col_scale[j:j + 1, :]
         stray = direction - M[here]
         M[here] = M[here] + (1.0 - first_decay) * stray
         return stray * stray
 
-    col_sum = sums(1, strays)
+    col_sum = sums(strays)
     row_all, col_all, total, _, drain1 = reduced(1, col_sum, [jnp.zeros((1, 2 * LANES), F32)], drain0)
     share = first_decay * first_decay
     row_conf_new = keep * states[2] + fresh * (row_all * (share / full_cols) + tiny_confidence)
@@ -416,7 +428,9 @@
             pltpu.VMEM((tokens, cols), out_grads.dtype),
             pltpu.VMEM((rows, cols), F32),
             pltpu.VMEM((4, 8, LANES), F32),
-            pltpu.VMEM((3, 8, LANES), F32),
+            pltpu.VMEM((rows, LANES), F32),
+            pltpu.VMEM((rows, LANES), F32),
+            pltpu.VMEM((2, 8, LANES), F32),
             pltpu.VMEM((2, C, 8, LANES), F32),
             pltpu.VMEM((2, 8, LANES), F32),
             pltpu.VMEM((2, R, 8, LANES), F32),

time: 86.8 us -> 83.7 us (0.964)
  Pallas kernels: 86.1 us -> 83 us
    pallas_call x1, Pallas kernels: 83 us -> 79.9 us  [on_device(): pl.pallas_call(functools.partial(kernel, R, C), out_shape=(pltpu.VMEM((ro...]
where the time goes in v4:
time: 83.7 us; the launch traced here: 83.6 us
  Pallas kernels  83 us (99%)
    pallas_call x1, Pallas kernels, on_device(): pl.pallas_call(functools.partial(kernel, R, C), out_shape=(pltpu.VMEM((ro...  79.9 us
    pallas_call x1, Pallas kernels, on_device(): pl.pallas_call(finish, out_shape=(big, big, by_row, by_col, by_row, by_co...  3.09 us

profile of v4, /device:TPU:1, one launch (start us, length us, event | category | flops | bytes accessed | tf_op | source)
XLA Modules:
  0.0 83.6 jit_solution(1812192953458712465)
XLA Ops:
  0.6 79.9 %came_step.1 = (f32[896,1024]{1,0:T(8,128)S(1)}, f32[6,8,128]{2,1,0:T(8,128)S(1)}) custom-call(bf16[512,896]{1,0:T(8,128)(2,1)} %acts.1, bf16[128,1024]{1,0:T(8,128)(2,1)} %grads.1, f32[896,1024]{1,0:T(8,128)} %moment.1, f32[7,128]{1,0:T(8,128)} %bitcast.8, f32[8,128]{1,0:T(8,128)} %bitcast.9, f32[7,128]{1,0:T(8,128)} %bitcast.10, f32[8,128]{1,0:T(8,128)} %bitcast.11), custom_call_target="tpu_custom_call" | custom-call | flops 7516192768 | bytes 31457280 | tf_op jit(solution)/shard_map/came_step/pallas_call | solution.py:421
  80.5 3.1 %finish.1 = (f32[896,1024]{1,0:T(8,128)}, f32[896,1024]{1,0:T(8,128)}, f32[7,128]{1,0:T(8,128)}, f32[8,128]{1,0:T(8,128)}, f32[7,128]{1,0:T(8,128)}, /*index=5*/f32[8,128]{1,0:T(8,128)}) custom-call(f32[896,1024]{1,0:T(8,128)S(1)} %get-tuple-element.14.M, f32[6,8,128]{2,1,0:T(8,128)S(1)} %get-tuple-element.15.packed), custom_call_target="tpu_custom_call" | custom-call | flops 1835008 | bytes 11010048 | tf_op jit(solution)/shard_map/finish/pallas_call | solution.py:452

commit v5 on v4

--- a/solution.py
+++ b/solution.py
@@ -22,8 +22,8 @@
 ORDER = (
     ("z", "Q", 0, 0), ("x", "P", 0, 0), ("x", "Q", 0, 0), ("z", "P", 0, 0), "own low",
     ("z", "P", 1, 0), ("x", "P", 0, 1), ("x", "Q", 1, 0), ("z", "Q", 0, 1), "own high",
-    ("x", "Q", -1, 0), ("z", "P", -1, 0), "strip", ("z", "P", 2, 0), ("x", "Q", 0, 1),
-    ("z", "Q", 0, 2), ("x", "Q", 2, 0), ("z", "P", 0, 1), ("x", "Q", 1, 1), "near",
+    ("x", "Q", -1, 0), ("z", "P", -1, 0), ("x", "Q", 0, 1), "strip out", ("z", "P", 0, 1),
+    ("z", "Q", 0, 2), ("x", "Q", 2, 0), ("x", "Q", 1, 1), "strip", ("z", "P", 2, 0), "near",
     ("z", "P", 1, 1), ("x", "Q", -2, 0), ("x", "Q", -1, 1), ("z", "Q", 0, 3), ("z", "P", -1, 1),
     ("x", "Q", 3, 0), ("z", "P", 2, 1), "cross",
     ("x", "Q", 2, 1), ("x", "Q", -3, 0), ("z", "P", 0, 2), ("z", "P", 1, 2), ("x", "Q", -2, 1),
@@ -63,7 +63,7 @@
     far, twin = rem(y + 2, Y) * 2 + core, y * 2 + 1 - core
 
     barrier = pltpu.get_barrier_semaphore()
-    for r in (*ring_to.values(), across):
+    for r in ring_to.values():
         pl.semaphore_signal(barrier, inc=1, device_id=(r, col), device_id_type=MESH)
     for c in (up, down, twin):
         pl.semaphore_signal(barrier, inc=1, device_id=(row, c), device_id_type=MESH)
@@ -80,7 +80,7 @@
     states[...] = jnp.zeros_like(states)
     for load in loads:
         load.start()
-    pl.semaphore_wait(barrier, 8)
+    pl.semaphore_wait(barrier, 7)
 
     def extent(message):
         axis, sign, kind, off, hops = message
@@ -111,13 +111,13 @@
         there = placed(message, hops)
         return pltpu.make_async_remote_copy(
             src_ref=grads.at[pl.ds(first, size)] if made == 0 and off == 0 else there, dst_ref=there,
-            send_sem=ring_send.at[lane, number], recv_sem=ring_recv.at[lane, number],
+            send_sem=ring_send.at[lane], recv_sem=ring_recv.at[lane, number],
             device_id=(ring_to[axis, sign], col), device_id_type=MESH)
 
     def strip(owner):
         return pltpu.make_async_remote_copy(
             src_ref=grads.at[pl.ds(p_rows, 16)], dst_ref=B.at[part(owner * tb + p_rows, 16, 16)],
-            send_sem=act_send.at[11], recv_sem=act_recv.at[11],
+            send_sem=act_send.at[1], recv_sem=act_recv.at[11],
             device_id=(across, col), device_id_type=MESH)
 
     sent, landed = [], set()
@@ -158,7 +158,7 @@
         there = A.at[part(owner * shard + first, hs, size)]
         return pltpu.make_async_remote_copy(
             src_ref=there if src is None else src, dst_ref=there,
-            send_sem=act_send.at[i], recv_sem=act_recv.at[i],
+            send_sem=act_send.at[0], recv_sem=act_recv.at[i],
             device_id=(row, to), device_id_type=MESH)
 
     low, high = acts.at[pl.ds(0, hs)], acts.at[pl.ds(hs, hs)]
@@ -181,7 +181,7 @@
     act_steps = {
         "own low": ((), (0, 3, 6)), "own high": ((), (1, 4)), "near": ((0, 3), (2, 5)),
         "cross": ((1, 4), (7, 8)), "far": ((2, 5), (9, 10)), "all": ((6, 7, 8, 9, 10), ()),
-        "strip": ((), ()),
+        "strip": ((), ()), "strip out": ((), ()),
     }
 
     def fours(i):
@@ -227,7 +227,8 @@
                 act_in[i].wait_recv()
             for i in leave:
                 act_out[i].start()
-            if entry == "own low":
+            if entry == "strip out":
+                await_messages([("x", s, "P", 0, 1) for s in (1, -1)])
                 strip(row).start()
             if entry == "strip":
                 strip(across).wait_recv()
@@ -244,36 +245,37 @@
 
     def exchange(phase, src, got, axis, send_sem, recv_sem):
         me, size = (row, R) if axis == "row" else (col, C)
-        steps = sorted(range(1, size), key=lambda i: -hops_to(axis, i))
-
-        def copy(i, source, target):
-            to = rem(me + i, size)
+
+        def from_far(k, length):
+            return length // 2 + div(k + 1, 2) * (2 * rem(k, 2) - 1)
+
+        def copy(k, source, target):
+            if axis == "row":
+                to = at_offset(from_far(div(k, X), Z), from_far(rem(k, X), X)), col
+            else:
+                to = row, rem(y + from_far(div(k, 2), Y), Y) * 2 + rem(core + 1 + k, 2)
             return pltpu.make_async_remote_copy(
                 src_ref=source, dst_ref=target,
                 send_sem=send_sem.at[phase], recv_sem=recv_sem.at[phase],
-                device_id=(to, col) if axis == "row" else (row, to), device_id_type=MESH)
+                device_id=to, device_id_type=MESH)
 
         others = got.at[phase, pl.ds(0, size - 1)]
 
         def start():
-            for i in steps:
-                copy(i, src, got.at[phase, me]).start()
+            def go(k, carry):
+                copy(k, src, got.at[phase, me]).start()
+                return carry
+            lax.fori_loop(0, size - 1, go, 0)
             got[phase, me] = src[...]
 
         def result():
-            copy(1, others, others).wait_recv()
+            copy(0, others, others).wait_recv()
             return jnp.sum(got[phase, pl.ds(0, size)], axis=0)
 
         def drain():
-            copy(1, others, others).wait_send()
+            copy(0, others, others).wait_send()
 
         return start, result, drain
-
-    def hops_to(axis, i):
-        if axis == "row":
-            dz, dx = i // X, i % X
-            return min(dz, Z - dz) + min(dx, X - dx)
-        return min(i // 2, Y - i // 2) + i % 2
 
     def whole(tile):
         return jnp.sum(tile, axis=(0, 1), keepdims=True)
@@ -334,10 +336,16 @@
         return g * g
 
     def gather_drain():
-        for message in sent:
-            ring(message, message[4]).wait_send()
-        for copy in act_out.values():
-            copy.wait_send()
+        for lane, (axis, sign) in enumerate(ring_to):
+            gone = sum(extent(m)[1] for m in sent if m[:2] == (axis, sign))
+            gone = B.at[pl.ds(0, gone)]
+            pltpu.make_async_remote_copy(
+                src_ref=gone, dst_ref=gone, send_sem=ring_send.at[lane], recv_sem=ring_recv.at[lane, 0],
+                device_id=(ring_to[axis, sign], col), device_id_type=MESH).wait_send()
+        gone = A.at[pl.ds(0, 7 * shard)]
+        pltpu.make_async_remote_copy(
+            src_ref=gone, dst_ref=gone, send_sem=act_send.at[0], recv_sem=act_recv.at[0],
+            device_id=(row, twin), device_id_type=MESH).wait_send()
         strip(row).wait_send()
 
     col_sum = sums(squared)
@@ -438,7 +446,7 @@
             pltpu.VMEM((2, R, 1, 3 * LANES), F32),
             pltpu.VMEM((2, 1, LANES), F32),
             pltpu.VMEM((2, C, 1, LANES), F32),
-            dma((4, 20)), dma((4, 20)), dma((12,)), dma((12,)), dma((7,)),
+            dma((4,)), dma((4, 20)), dma((2,)), dma((12,)), dma((7,)),
             dma((2,)), dma((2,)), dma((2,)), dma((2,)), dma((2,)), dma((2,)), dma((2,)), dma((2,)),
         ],
         compiler_params=pltpu.CompilerParams(

time: 83.7 us -> 84 us (level)
  no operation moved by 1% of the time
where the time goes in v5:
time: 84 us; the launch traced here: 83.9 us
  Pallas kernels  83.3 us (99%)
    pallas_call x1, Pallas kernels, on_device(): pl.pallas_call(functools.partial(kernel, R, C), out_shape=(pltpu.VMEM((ro...  80.2 us
    pallas_call x1, Pallas kernels, on_device(): pl.pallas_call(finish, out_shape=(big, big, by_row, by_col, by_row, by_co...  3.09 us

profile of v5, /device:TPU:1, one launch (start us, length us, event | category | flops | bytes accessed | tf_op | source)
XLA Modules:
  0.0 83.9 jit_solution(11607768736334913119)
XLA Ops:
  0.6 80.2 %came_step.1 = (f32[896,1024]{1,0:T(8,128)S(1)}, f32[6,8,128]{2,1,0:T(8,128)S(1)}) custom-call(bf16[512,896]{1,0:T(8,128)(2,1)} %acts.1, bf16[128,1024]{1,0:T(8,128)(2,1)} %grads.1, f32[896,1024]{1,0:T(8,128)} %moment.1, f32[7,128]{1,0:T(8,128)} %bitcast.8, f32[8,128]{1,0:T(8,128)} %bitcast.9, f32[7,128]{1,0:T(8,128)} %bitcast.10, f32[8,128]{1,0:T(8,128)} %bitcast.11), custom_call_target="tpu_custom_call" | custom-call | flops 7516192768 | bytes 31457280 | tf_op jit(solution)/shard_map/came_step/pallas_call | solution.py:429
  80.9 3.1 %finish.1 = (f32[896,1024]{1,0:T(8,128)}, f32[896,1024]{1,0:T(8,128)}, f32[7,128]{1,0:T(8,128)}, f32[8,128]{1,0:T(8,128)}, f32[7,128]{1,0:T(8,128)}, /*index=5*/f32[8,128]{1,0:T(8,128)}) custom-call(f32[896,1024]{1,0:T(8,128)S(1)} %get-tuple-element.14.M, f32[6,8,128]{2,1,0:T(8,128)S(1)} %get-tuple-element.15.packed), custom_call_target="tpu_custom_call" | custom-call | flops 1835008 | bytes 11010048 | tf_op jit(solution)/shard_map/finish/pallas_call | solution.py:460

commit v6 on v5

--- a/solution.py
+++ b/solution.py
@@ -27,10 +27,11 @@
     ("z", "P", 1, 1), ("x", "Q", -2, 0), ("x", "Q", -1, 1), ("z", "Q", 0, 3), ("z", "P", -1, 1),
     ("x", "Q", 3, 0), ("z", "P", 2, 1), "cross",
     ("x", "Q", 2, 1), ("x", "Q", -3, 0), ("z", "P", 0, 2), ("z", "P", 1, 2), ("x", "Q", -2, 1),
-    ("z", "P", -1, 2), ("x", "Q", 4, 0), ("z", "P", 2, 2), "far", ("x", "Q", 3, 1), ("z", "P", 0, 3), "all",
+    ("z", "P", -1, 2), ("x", "Q", 4, 0), "far", ("z", "P", 2, 2), ("x", "Q", 3, 1), "all",
 )
-FOURS_ORDER = ((), (("x", "Q", -3, 1),), (("z", "P", 1, 3),), (("z", "P", -1, 3),), (), (("x", "Q", 4, 1),))
-TWOS_ORDER = ((("z", "P", 2, 3),), (), (), ())
+FOURS_ORDER = (
+    (), (("z", "P", 0, 3),), (), (("x", "Q", -3, 1), ("z", "P", 1, 3)), (), (("z", "P", -1, 3),))
+TWOS_ORDER = ((), (("x", "Q", 4, 1), ("z", "P", 2, 3)), (), ())
 HOPS = {"z": 4, "x": 2}
 
 

time: 84 us -> 83 us (0.988)
  Pallas kernels: 83.3 us -> 82.3 us
    pallas_call x1, Pallas kernels: 80.2 us -> 79.2 us  [on_device(): pl.pallas_call(functools.partial(kernel, R, C), out_shape=(pltpu.VMEM((ro...]
where the time goes in v6:
time: 83 us; the launch traced here: 82.9 us
  Pallas kernels  82.3 us (99%)
    pallas_call x1, Pallas kernels, on_device(): pl.pallas_call(functools.partial(kernel, R, C), out_shape=(pltpu.VMEM((ro...  79.2 us
    pallas_call x1, Pallas kernels, on_device(): pl.pallas_call(finish, out_shape=(big, big, by_row, by_col, by_row, by_co...  3.09 us

profile of v6, /device:TPU:1, one launch (start us, length us, event | category | flops | bytes accessed | tf_op | source)
XLA Modules:
  0.0 82.9 jit_solution(3778496898178133140)
XLA Ops:
  0.6 79.2 %came_step.1 = (f32[896,1024]{1,0:T(8,128)S(1)}, f32[6,8,128]{2,1,0:T(8,128)S(1)}) custom-call(bf16[512,896]{1,0:T(8,128)(2,1)} %acts.1, bf16[128,1024]{1,0:T(8,128)(2,1)} %grads.1, f32[896,1024]{1,0:T(8,128)} %moment.1, f32[7,128]{1,0:T(8,128)} %bitcast.8, f32[8,128]{1,0:T(8,128)} %bitcast.9, f32[7,128]{1,0:T(8,128)} %bitcast.10, f32[8,128]{1,0:T(8,128)} %bitcast.11), custom_call_target="tpu_custom_call" | custom-call | flops 7516192768 | bytes 31457280 | tf_op jit(solution)/shard_map/came_step/pallas_call | solution.py:430
  79.8 3.1 %finish.1 = (f32[896,1024]{1,0:T(8,128)}, f32[896,1024]{1,0:T(8,128)}, f32[7,128]{1,0:T(8,128)}, f32[8,128]{1,0:T(8,128)}, f32[7,128]{1,0:T(8,128)}, /*index=5*/f32[8,128]{1,0:T(8,128)}) custom-call(f32[896,1024]{1,0:T(8,128)S(1)} %get-tuple-element.14.M, f32[6,8,128]{2,1,0:T(8,128)S(1)} %get-tuple-element.15.packed), custom_call_target="tpu_custom_call" | custom-call | flops 1835008 | bytes 11010048 | tf_op jit(solution)/shard_map/finish/pallas_call | solution.py:461

commit v7 on v6

--- a/solution.py
+++ b/solution.py
@@ -36,9 +36,10 @@
 
 
 def kernel(R, C, acts, grads, moment, row_state, col_state, row_conf, col_conf, M, packed,
-           A, B, G, states, row_sums, row_scale, row_part, row_got, col_part, col_got, tot_part, tot_got, all_part, all_got,
+           A, B, G, states, row_sums, row_scale, row_part, row_got, col_part, x_got, z_part, col_got,
+           tot_part, tot_got, all_part, all_got,
            ring_send, ring_recv, act_send, act_recv, load_sem,
-           row_send, row_recv, col_send, col_recv, tot_send, tot_recv, all_send, all_recv):
+           row_send, row_recv, x_send, x_recv, col_send, col_recv, tot_send, tot_recv, all_send, all_recv, known):
     Z, Y = R // X, C // 2
     row, col = lax.axis_index("row"), lax.axis_index("col")
     div, rem = lax.div, lax.rem
@@ -62,6 +63,42 @@
     ring_to = {("z", s): at_offset(s, 0) for s in (1, -1)} | {("x", s): at_offset(0, s) for s in (1, -1)}
     up, down = rem(y + 1, Y) * 2 + core, rem(y + Y - 1, Y) * 2 + core
     far, twin = rem(y + 2, Y) * 2 + core, y * 2 + 1 - core
+
+    def whole(tile):
+        return jnp.sum(tile, axis=(0, 1), keepdims=True)
+
+    def from_far(length):
+        return sorted(range(length), key=lambda d: -min(d, length - d))
+
+    def to_twin(go):
+        go((row, twin))
+
+    def to_x(go):
+        for dx in from_far(X)[:-1]:
+            go((at_offset(0, dx), col))
+
+    def to_z(go):
+        for dz in from_far(Z)[:-1]:
+            go((at_offset(dz, 0), col))
+
+    def to_col(go):
+        for dy in from_far(Y):
+            for dc in (1, 0):
+                if dy or dc:
+                    go((row, rem(y + dy, Y) * 2 + rem(core + dc, 2)))
+
+    def to_chips(go):
+        def plane(a, carry):
+            dz = Z // 2 + div(a + 1, 2) * (2 * rem(a, 2) - 1)
+            for dx in from_far(X):
+                for dy in from_far(Y):
+                    to = at_offset(dz, dx), rem(y + dy, Y) * 2 + core
+                    if dx or dy:
+                        go(to)
+                    else:
+                        pl.when(a < Z - 1)(functools.partial(go, to))
+            return carry
+        lax.fori_loop(0, Z, plane, 0)
 
     barrier = pltpu.get_barrier_semaphore()
     for r in ring_to.values():
@@ -239,47 +276,41 @@
                 G[...] = jnp.zeros_like(G)
         else:
             send(*entry)
-    add_products(fours, FOURS_ORDER)
-    add_products(twos, TWOS_ORDER)
+    to_z(lambda to: pl.semaphore_signal(known.at[0], inc=1, device_id=to, device_id_type=MESH))
     for load in loads[2:]:
         load.wait()
-
-    def exchange(phase, src, got, axis, send_sem, recv_sem):
-        me, size = (row, R) if axis == "row" else (col, C)
-
-        def from_far(k, length):
-            return length // 2 + div(k + 1, 2) * (2 * rem(k, 2) - 1)
-
-        def copy(k, source, target):
-            if axis == "row":
-                to = at_offset(from_far(div(k, X), Z), from_far(rem(k, X), X)), col
-            else:
-                to = row, rem(y + from_far(div(k, 2), Y), Y) * 2 + rem(core + 1 + k, 2)
+    col_part[...] = jnp.zeros_like(col_part)
+    row_part[...] = jnp.zeros_like(row_part)
+    lane_ids = lax.broadcasted_iota(jnp.int32, (1, LANES), 1)
+    states_sums = [whole(states[k]) for k in (0, 2)]
+    add_products(fours, FOURS_ORDER)
+    pl.semaphore_wait(known.at[0], Z - 1)
+    to_x(lambda to: pl.semaphore_signal(known.at[1], inc=1, device_id=to, device_id_type=MESH))
+    add_products(twos, TWOS_ORDER)
+    pl.semaphore_wait(known.at[1], X - 1)
+    def exchange(phase, src, got, slot, to_each, sems):
+        send_sem, recv_sem = sems
+
+        def copy(source, target, to):
             return pltpu.make_async_remote_copy(
                 src_ref=source, dst_ref=target,
                 send_sem=send_sem.at[phase], recv_sem=recv_sem.at[phase],
                 device_id=to, device_id_type=MESH)
 
-        others = got.at[phase, pl.ds(0, size - 1)]
+        others = got.at[phase, pl.ds(0, got.shape[1] - 1)]
 
         def start():
-            def go(k, carry):
-                copy(k, src, got.at[phase, me]).start()
-                return carry
-            lax.fori_loop(0, size - 1, go, 0)
-            got[phase, me] = src[...]
+            to_each(lambda to: copy(src, got.at[phase, slot], to).start())
+            got[phase, slot] = src[...]
 
         def result():
-            copy(0, others, others).wait_recv()
-            return jnp.sum(got[phase, pl.ds(0, size)], axis=0)
+            copy(others, others, (row, twin)).wait_recv()
+            return jnp.sum(got[phase], axis=0)
 
         def drain():
-            copy(0, others, others).wait_send()
+            copy(others, others, (row, twin)).wait_send()
 
         return start, result, drain
-
-    def whole(tile):
-        return jnp.sum(tile, axis=(0, 1), keepdims=True)
 
     def sums(block):
         def rows_of(i, col_sum):
@@ -298,39 +329,38 @@
     def reduced(phase, col_sum, beside, meanwhile):
         col_sum = jnp.sum(col_sum, axis=0, keepdims=True)
         col_sums = [col_sum[:, j * LANES:(j + 1) * LANES] for j in range(nc)]
-        tot_part[phase] = jnp.concatenate([functools.reduce(jnp.add, col_sums)] + beside, 1)
-        by_tot = exchange(phase, tot_part.at[phase], tot_got, "row", tot_send, tot_recv)
-        by_tot[0]()
+        values = whole(functools.reduce(jnp.add, col_sums))
+        for lane, value in enumerate(beside):
+            values = jnp.where(lane_ids == lane + 1, value, values)
+        tot_part[phase] = jnp.broadcast_to(values, (1, LANES))
+        by_twin = exchange(phase, tot_part.at[phase], tot_got, core, to_twin, (tot_send, tot_recv))
+        by_twin[0]()
         for j in range(nc):
             col_part[phase, j:j + 1, :] = col_sums[j]
-        by_col = exchange(phase, col_part.at[phase], col_got, "row", col_send, col_recv)
-        by_row = exchange(phase, row_part.at[phase], row_got, "col", row_send, row_recv)
-        by_col[0]()
+        by_x = exchange(phase, col_part.at[phase], x_got, x, to_x, (x_send, x_recv))
+        by_x[0]()
         for i in range(nr):
             turned = row_sums[i * LANES:(i + 1) * LANES, :].T
             row_part[phase, i:i + 1, :] = jnp.sum(turned, axis=0, keepdims=True)
+        by_row = exchange(phase, row_part.at[phase], row_got, col, to_col, (row_send, row_recv))
         by_row[0]()
+        all_part[phase] = by_twin[1]()
+        by_all = exchange(phase, all_part.at[phase], all_got, row * Y + y, to_chips, (all_send, all_recv))
+        by_all[0]()
+        z_part[phase] = by_x[1]()
+        by_z = exchange(phase, z_part.at[phase], col_got, z, to_z, (col_send, col_recv))
+        by_z[0]()
         meanwhile()
-        tot_rows = by_tot[1]()
-        all_part[phase] = tot_rows[:, :LANES]
-        by_all = exchange(phase, all_part.at[phase], all_got, "col", all_send, all_recv)
-        by_all[0]()
-        col_all = by_col[1]()
         row_all = by_row[1]()
-        for one in (by_tot, by_col, by_row):
+        col_all = by_z[1]()
+        for one in (by_twin, by_x, by_row, by_z):
             one[2]()
-        total = whole(by_all[1]())
-
-        def drain():
-            by_all[2]()
-        return row_all, col_all, total, tot_rows, drain
+        totals = by_all[1]()
+        return row_all, col_all, totals, by_all[2]
 
     def down_rows(factors):
         for i in range(nr):
             row_scale[i * LANES:(i + 1) * LANES, :] = jnp.broadcast_to(factors[i:i + 1, :], (LANES, LANES)).T
-
-    col_part[...] = jnp.zeros_like(col_part)
-    row_part[...] = jnp.zeros_like(row_part)
 
     def squared(at, j):
         g = G[at, j * LANES:(j + 1) * LANES]
@@ -350,9 +380,8 @@
         strip(row).wait_send()
 
     col_sum = sums(squared)
-    states_sums = [jnp.sum(states[k], axis=0, keepdims=True) for k in (0, 2)]
-    row_all, col_all, total, tot_rows, drain0 = reduced(0, col_sum, states_sums, gather_drain)
-    row_state_sum, row_conf_sum = whole(tot_rows[:, LANES:2 * LANES]), whole(tot_rows[:, 2 * LANES:])
+    row_all, col_all, totals, drain0 = reduced(0, col_sum, states_sums, gather_drain)
+    total, row_state_sum, row_conf_sum = totals[:, 0:1], totals[:, 1:2] * (1.0 / C), totals[:, 2:3] * (1.0 / C)
     spread = jnp.minimum(1.0, (full_rows * full_cols) / (total + 1e-06))
     keep, fresh = second_decay, 1.0 - second_decay
     row_new = keep * states[0] + fresh * (spread * row_all * (1.0 / full_cols) + tiny_moment)
@@ -372,7 +401,8 @@
         return stray * stray
 
     col_sum = sums(strays)
-    row_all, col_all, total, _, drain1 = reduced(1, col_sum, [jnp.zeros((1, 2 * LANES), F32)], drain0)
+    row_all, col_all, totals, drain1 = reduced(1, col_sum, [], drain0)
+    total = totals[:, 0:1]
     share = first_decay * first_decay
     row_conf_new = keep * states[2] + fresh * (row_all * (share / full_cols) + tiny_confidence)
     col_conf_new = keep * states[3] + fresh * (col_all * (share / full_rows) + tiny_confidence)
@@ -442,13 +472,15 @@
             pltpu.VMEM((2, 8, LANES), F32),
             pltpu.VMEM((2, C, 8, LANES), F32),
             pltpu.VMEM((2, 8, LANES), F32),
-            pltpu.VMEM((2, R, 8, LANES), F32),
-            pltpu.VMEM((2, 1, 3 * LANES), F32),
-            pltpu.VMEM((2, R, 1, 3 * LANES), F32),
+            pltpu.VMEM((2, X, 8, LANES), F32),
+            pltpu.VMEM((2, 8, LANES), F32),
+            pltpu.VMEM((2, R // X, 8, LANES), F32),
             pltpu.VMEM((2, 1, LANES), F32),
-            pltpu.VMEM((2, C, 1, LANES), F32),
+            pltpu.VMEM((2, 2, 1, LANES), F32),
+            pltpu.VMEM((2, 1, LANES), F32),
+            pltpu.VMEM((2, R * C // 2, 1, LANES), F32),
             dma((4,)), dma((4, 20)), dma((2,)), dma((12,)), dma((7,)),
-            dma((2,)), dma((2,)), dma((2,)), dma((2,)), dma((2,)), dma((2,)), dma((2,)), dma((2,)),
+            *[dma((2,))] * 10, pltpu.SemaphoreType.REGULAR((2,)),
         ],
         compiler_params=pltpu.CompilerParams(
             collective_id=0, has_side_effects=True, vmem_limit_bytes=40 * 2**20),

time: 83 us -> 80.3 us (0.967)
  Pallas kernels: 82.3 us -> 79.6 us
    pallas_call x1, Pallas kernels: 79.2 us -> 76.5 us  [on_device(): pl.pallas_call(functools.partial(kernel, R, C), out_shape=(pltpu.VMEM((ro...]
where the time goes in v7:
time: 80.3 us
  Pallas kernels  79.6 us (99%)
    pallas_call x1, Pallas kernels, on_device(): pl.pallas_call(functools.partial(kernel, R, C), out_shape=(pltpu.VMEM((ro...  76.5 us
    pallas_call x1, Pallas kernels, on_device(): pl.pallas_call(finish, out_shape=(big, big, by_row, by_col, by_row, by_co...  3.09 us

profile of v7, /device:TPU:1, one launch (start us, length us, event | category | flops | bytes accessed | tf_op | source)
XLA Modules:
  0.0 80.3 jit_solution(15135545582505106386)
XLA Ops:
  0.6 76.5 %came_step.1 = (f32[896,1024]{1,0:T(8,128)S(1)}, f32[6,8,128]{2,1,0:T(8,128)S(1)}) custom-call(bf16[512,896]{1,0:T(8,128)(2,1)} %acts.1, bf16[128,1024]{1,0:T(8,128)(2,1)} %grads.1, f32[896,1024]{1,0:T(8,128)} %moment.1, f32[7,128]{1,0:T(8,128)} %bitcast.8, f32[8,128]{1,0:T(8,128)} %bitcast.9, f32[7,128]{1,0:T(8,128)} %bitcast.10, f32[8,128]{1,0:T(8,128)} %bitcast.11), custom_call_target="tpu_custom_call" | custom-call | flops 7516192768 | bytes 31457280 | tf_op jit(solution)/shard_map/came_step/pallas_call | solution.py:460
  77.2 3.1 %finish.1 = (f32[896,1024]{1,0:T(8,128)}, f32[896,1024]{1,0:T(8,128)}, f32[7,128]{1,0:T(8,128)}, f32[8,128]{1,0:T(8,128)}, f32[7,128]{1,0:T(8,128)}, /*index=5*/f32[8,128]{1,0:T(8,128)}) custom-call(f32[896,1024]{1,0:T(8,128)S(1)} %get-tuple-element.14.M, f32[6,8,128]{2,1,0:T(8,128)S(1)} %get-tuple-element.15.packed), custom_call_target="tpu_custom_call" | custom-call | flops 1835008 | bytes 11010048 | tf_op jit(solution)/shard_map/finish/pallas_call | solution.py:493

commit v8 on v7

--- a/solution.py
+++ b/solution.py
@@ -31,7 +31,7 @@
 )
 FOURS_ORDER = (
     (), (("z", "P", 0, 3),), (), (("x", "Q", -3, 1), ("z", "P", 1, 3)), (), (("z", "P", -1, 3),))
-TWOS_ORDER = ((), (("x", "Q", 4, 1), ("z", "P", 2, 3)), (), ())
+TWOS_ORDER = ((("x", "Q", 4, 1), ("z", "P", 2, 3)), (), (), ())
 HOPS = {"z": 4, "x": 2}
 
 
@@ -327,7 +327,6 @@
         return lax.fori_loop(0, nr, rows_of, jnp.zeros((8, cols), F32))
 
     def reduced(phase, col_sum, beside, meanwhile):
-        col_sum = jnp.sum(col_sum, axis=0, keepdims=True)
         col_sums = [col_sum[:, j * LANES:(j + 1) * LANES] for j in range(nc)]
         values = whole(functools.reduce(jnp.add, col_sums))
         for lane, value in enumerate(beside):
@@ -336,7 +335,7 @@
         by_twin = exchange(phase, tot_part.at[phase], tot_got, core, to_twin, (tot_send, tot_recv))
         by_twin[0]()
         for j in range(nc):
-            col_part[phase, j:j + 1, :] = col_sums[j]
+            col_part[phase, j:j + 1, :] = jnp.sum(col_sums[j], axis=0, keepdims=True)
         by_x = exchange(phase, col_part.at[phase], x_got, x, to_x, (x_send, x_recv))
         by_x[0]()
         for i in range(nr):

time: 80.3 us -> 79.7 us (level)
  no operation moved by 1% of the time
where the time goes in v8:
time: 79.7 us
  Pallas kernels  79 us (99%)
    pallas_call x1, Pallas kernels, on_device(): pl.pallas_call(functools.partial(kernel, R, C), out_shape=(pltpu.VMEM((ro...  75.9 us
    pallas_call x1, Pallas kernels, on_device(): pl.pallas_call(finish, out_shape=(big, big, by_row, by_col, by_row, by_co...  3.09 us

profile of v8, /device:TPU:1, one launch (start us, length us, event | category | flops | bytes accessed | tf_op | source)
XLA Modules:
  0.0 79.7 jit_solution(13729344776598109477)
XLA Ops:
  0.6 75.9 %came_step.1 = (f32[896,1024]{1,0:T(8,128)S(1)}, f32[6,8,128]{2,1,0:T(8,128)S(1)}) custom-call(bf16[512,896]{1,0:T(8,128)(2,1)} %acts.1, bf16[128,1024]{1,0:T(8,128)(2,1)} %grads.1, f32[896,1024]{1,0:T(8,128)} %moment.1, f32[7,128]{1,0:T(8,128)} %bitcast.8, f32[8,128]{1,0:T(8,128)} %bitcast.9, f32[7,128]{1,0:T(8,128)} %bitcast.10, f32[8,128]{1,0:T(8,128)} %bitcast.11), custom_call_target="tpu_custom_call" | custom-call | flops 7516192768 | bytes 31457280 | tf_op jit(solution)/shard_map/came_step/pallas_call | solution.py:459
  76.6 3.1 %finish.1 = (f32[896,1024]{1,0:T(8,128)}, f32[896,1024]{1,0:T(8,128)}, f32[7,128]{1,0:T(8,128)}, f32[8,128]{1,0:T(8,128)}, f32[7,128]{1,0:T(8,128)}, /*index=5*/f32[8,128]{1,0:T(8,128)}) custom-call(f32[896,1024]{1,0:T(8,128)S(1)} %get-tuple-element.14.M, f32[6,8,128]{2,1,0:T(8,128)S(1)} %get-tuple-element.15.packed), custom_call_target="tpu_custom_call" | custom-call | flops 1835008 | bytes 11010048 | tf_op jit(solution)/shard_map/finish/pallas_call | solution.py:492

commit v9 on v8

--- a/solution.py
+++ b/solution.py
@@ -36,7 +36,7 @@
 
 
 def kernel(R, C, acts, grads, moment, row_state, col_state, row_conf, col_conf, M, packed,
-           A, B, G, states, row_sums, row_scale, row_part, row_got, col_part, x_got, z_part, col_got,
+           A, B, G, states, row_sums, row_scale, row_part, row_got, col_part, x_got, x_part, col_got,
            tot_part, tot_got, all_part, all_got,
            ring_send, ring_recv, act_send, act_recv, load_sem,
            row_send, row_recv, x_send, x_recv, col_send, col_recv, tot_send, tot_recv, all_send, all_recv, known):
@@ -336,8 +336,8 @@
         by_twin[0]()
         for j in range(nc):
             col_part[phase, j:j + 1, :] = jnp.sum(col_sums[j], axis=0, keepdims=True)
-        by_x = exchange(phase, col_part.at[phase], x_got, x, to_x, (x_send, x_recv))
-        by_x[0]()
+        by_z = exchange(phase, col_part.at[phase], col_got, z, to_z, (col_send, col_recv))
+        by_z[0]()
         for i in range(nr):
             turned = row_sums[i * LANES:(i + 1) * LANES, :].T
             row_part[phase, i:i + 1, :] = jnp.sum(turned, axis=0, keepdims=True)
@@ -346,13 +346,13 @@
         all_part[phase] = by_twin[1]()
         by_all = exchange(phase, all_part.at[phase], all_got, row * Y + y, to_chips, (all_send, all_recv))
         by_all[0]()
-        z_part[phase] = by_x[1]()
-        by_z = exchange(phase, z_part.at[phase], col_got, z, to_z, (col_send, col_recv))
-        by_z[0]()
+        x_part[phase] = by_z[1]()
+        by_x = exchange(phase, x_part.at[phase], x_got, x, to_x, (x_send, x_recv))
+        by_x[0]()
         meanwhile()
         row_all = by_row[1]()
-        col_all = by_z[1]()
-        for one in (by_twin, by_x, by_row, by_z):
+        col_all = by_x[1]()
+        for one in (by_twin, by_z, by_row, by_x):
             one[2]()
         totals = by_all[1]()
         return row_all, col_all, totals, by_all[2]

time: 79.7 us -> 79.8 us (level)
  no operation moved by 1% of the time
where the time goes in v9:
time: 79.8 us; the launch traced here: 79.7 us
  Pallas kernels  79.1 us (99%)
    pallas_call x1, Pallas kernels, on_device(): pl.pallas_call(functools.partial(kernel, R, C), out_shape=(pltpu.VMEM((ro...  76 us
    pallas_call x1, Pallas kernels, on_device(): pl.pallas_call(finish, out_shape=(big, big, by_row, by_col, by_row, by_co...  3.09 us

profile of v9, /device:TPU:1, one launch (start us, length us, event | category | flops | bytes accessed | tf_op | source)
XLA Modules:
  0.0 79.7 jit_solution(2436851800096549386)
XLA Ops:
  0.6 76.0 %came_step.1 = (f32[896,1024]{1,0:T(8,128)S(1)}, f32[6,8,128]{2,1,0:T(8,128)S(1)}) custom-call(bf16[512,896]{1,0:T(8,128)(2,1)} %acts.1, bf16[128,1024]{1,0:T(8,128)(2,1)} %grads.1, f32[896,1024]{1,0:T(8,128)} %moment.1, f32[7,128]{1,0:T(8,128)} %bitcast.8, f32[8,128]{1,0:T(8,128)} %bitcast.9, f32[7,128]{1,0:T(8,128)} %bitcast.10, f32[8,128]{1,0:T(8,128)} %bitcast.11), custom_call_target="tpu_custom_call" | custom-call | flops 7516192768 | bytes 31457280 | tf_op jit(solution)/shard_map/came_step/pallas_call | solution.py:459
  76.6 3.1 %finish.1 = (f32[896,1024]{1,0:T(8,128)}, f32[896,1024]{1,0:T(8,128)}, f32[7,128]{1,0:T(8,128)}, f32[8,128]{1,0:T(8,128)}, f32[7,128]{1,0:T(8,128)}, /*index=5*/f32[8,128]{1,0:T(8,128)}) custom-call(f32[896,1024]{1,0:T(8,128)S(1)} %get-tuple-element.14.M, f32[6,8,128]{2,1,0:T(8,128)S(1)} %get-tuple-element.15.packed), custom_call_target="tpu_custom_call" | custom-call | flops 1835008 | bytes 11010048 | tf_op jit(solution)/shard_map/finish/pallas_call | solution.py:492

commit v10 on v9

--- a/solution.py
+++ b/solution.py
@@ -106,30 +106,18 @@
     for c in (up, down, twin):
         pl.semaphore_signal(barrier, inc=1, device_id=(row, c), device_id_type=MESH)
 
-    loads = [
-        pltpu.make_async_copy(grads, B.at[part(row * tb, tb, tb)], load_sem.at[0]),
-        pltpu.make_async_copy(acts, A.at[part(col * shard, shard, shard)], load_sem.at[1]),
-        pltpu.make_async_copy(moment, M, load_sem.at[2]),
-        pltpu.make_async_copy(row_state, states.at[0, pl.ds(0, nr)], load_sem.at[3]),
-        pltpu.make_async_copy(col_state, states.at[1, pl.ds(0, nc)], load_sem.at[4]),
-        pltpu.make_async_copy(row_conf, states.at[2, pl.ds(0, nr)], load_sem.at[5]),
-        pltpu.make_async_copy(col_conf, states.at[3, pl.ds(0, nc)], load_sem.at[6]),
-    ]
-    states[...] = jnp.zeros_like(states)
-    for load in loads:
-        load.start()
     pl.semaphore_wait(barrier, 7)
 
     def extent(message):
         axis, sign, kind, off, hops = message
         first, size = (0, p_rows) if kind == "P" else (p_rows, tb - p_rows)
-        if axis == "z" and kind == "P" and off == HOPS["x"]:
+        if axis == "z" and kind == "P" and off == HOPS["x"] and hops < HOPS["z"] - 1:
             size += 16
-        if axis == "x" and kind == "Q" and hops == HOPS["x"] - 1:
+        if axis == "x" and kind == "Q" and hops == HOPS["x"] - 1 and off != HOPS["z"]:
             first, size = first + 16, size - 16
         if hops == HOPS[axis] - 1:
             low = (size // 2 + 15) // 16 * 16
-            low = size - low if off % 2 else low
+            low = size - low if off % 2 or off == HOPS["z"] else low
             return (first, low) if sign > 0 else (first + low, size - low)
         return first, size
 
@@ -258,6 +246,15 @@
             return (dz, 0), (dz, 1), (dz, 3), (dz - 6 * odd, 2 - 2 * odd)
         return (5 - 2 * (n % 2) + n // 3, 1 + (n + 1) // 2), (5 - (n + 2) // 3, n - 1)
 
+    loads = [
+        pltpu.make_async_copy(grads, B.at[part(row * tb, tb, tb)], load_sem.at[0]),
+        pltpu.make_async_copy(acts, A.at[part(col * shard, shard, shard)], load_sem.at[1]),
+        pltpu.make_async_copy(moment, M, load_sem.at[2]),
+        pltpu.make_async_copy(row_state, states.at[0, pl.ds(0, nr)], load_sem.at[3]),
+        pltpu.make_async_copy(col_state, states.at[1, pl.ds(0, nc)], load_sem.at[4]),
+        pltpu.make_async_copy(row_conf, states.at[2, pl.ds(0, nr)], load_sem.at[5]),
+        pltpu.make_async_copy(col_conf, states.at[3, pl.ds(0, nc)], load_sem.at[6]),
+    ]
     for entry in ORDER:
         if isinstance(entry, str):
             arrive, leave = act_steps[entry]
@@ -270,6 +267,10 @@
                 strip(row).start()
             if entry == "strip":
                 strip(across).wait_recv()
+            if entry == "own low":
+                states[...] = jnp.zeros_like(states)
+                for load in loads:
+                    load.start()
             if entry == "own high":
                 loads[0].wait()
                 loads[1].wait()

time: 79.8 us -> 79.8 us (level)
  no operation moved by 1% of the time
where the time goes in v10:
time: 79.8 us; the launch traced here: 79.7 us
  Pallas kernels  79 us (99%)
    pallas_call x1, Pallas kernels, on_device(): pl.pallas_call(functools.partial(kernel, R, C), out_shape=(pltpu.VMEM((ro...  75.9 us
    pallas_call x1, Pallas kernels, on_device(): pl.pallas_call(finish, out_shape=(big, big, by_row, by_col, by_row, by_co...  3.09 us

profile of v10, /device:TPU:1, one launch (start us, length us, event | category | flops | bytes accessed | tf_op | source)
XLA Modules:
  0.0 79.7 jit_solution(16768366271420095511)
XLA Ops:
  0.6 75.9 %came_step.1 = (f32[896,1024]{1,0:T(8,128)S(1)}, f32[6,8,128]{2,1,0:T(8,128)S(1)}) custom-call(bf16[512,896]{1,0:T(8,128)(2,1)} %acts.1, bf16[128,1024]{1,0:T(8,128)(2,1)} %grads.1, f32[896,1024]{1,0:T(8,128)} %moment.1, f32[7,128]{1,0:T(8,128)} %bitcast.8, f32[8,128]{1,0:T(8,128)} %bitcast.9, f32[7,128]{1,0:T(8,128)} %bitcast.10, f32[8,128]{1,0:T(8,128)} %bitcast.11), custom_call_target="tpu_custom_call" | custom-call | flops 7516192768 | bytes 31457280 | tf_op jit(solution)/shard_map/came_step/pallas_call | solution.py:460
  76.6 3.1 %finish.1 = (f32[896,1024]{1,0:T(8,128)}, f32[896,1024]{1,0:T(8,128)}, f32[7,128]{1,0:T(8,128)}, f32[8,128]{1,0:T(8,128)}, f32[7,128]{1,0:T(8,128)}, /*index=5*/f32[8,128]{1,0:T(8,128)}) custom-call(f32[896,1024]{1,0:T(8,128)S(1)} %get-tuple-element.14.M, f32[6,8,128]{2,1,0:T(8,128)S(1)} %get-tuple-element.15.packed), custom_call_target="tpu_custom_call" | custom-call | flops 1835008 | bytes 11010048 | tf_op jit(solution)/shard_map/finish/pallas_call | solution.py:493

commit v11 on v9

--- a/solution.py
+++ b/solution.py
@@ -36,7 +36,7 @@
 
 
 def kernel(R, C, acts, grads, moment, row_state, col_state, row_conf, col_conf, M, packed,
-           A, B, G, states, row_sums, row_scale, row_part, row_got, col_part, x_got, x_part, col_got,
+           A, B, G, states, col_acc, row_sums, row_scale, row_part, row_got, col_part, x_got, x_part, col_got,
            tot_part, tot_got, all_part, all_got,
            ring_send, ring_recv, act_send, act_recv, load_sem,
            row_send, row_recv, x_send, x_recv, col_send, col_recv, tot_send, tot_recv, all_send, all_recv, known):
@@ -326,12 +326,46 @@
 
         return lax.fori_loop(0, nr, rows_of, jnp.zeros((8, cols), F32))
 
-    def reduced(phase, col_sum, beside, meanwhile):
-        col_sums = [col_sum[:, j * LANES:(j + 1) * LANES] for j in range(nc)]
+    def squared(at, j):
+        g = G[at, j * LANES:(j + 1) * LANES]
+        return g * g
+
+    def strays(at, j):
+        here = (at, slice(j * LANES, (j + 1) * LANES))
+        direction = G[here] * row_scale[at, :] * packed[5, j:j + 1, :]
+        stray = direction - M[here]
+        M[here] = M[here] + (1.0 - first_decay) * stray
+        return stray * stray
+
+    def gather_drain():
+        for lane, (axis, sign) in enumerate(ring_to):
+            gone = sum(extent(m)[1] for m in sent if m[:2] == (axis, sign))
+            gone = B.at[pl.ds(0, gone)]
+            pltpu.make_async_remote_copy(
+                src_ref=gone, dst_ref=gone, send_sem=ring_send.at[lane], recv_sem=ring_recv.at[lane, 0],
+                device_id=(ring_to[axis, sign], col), device_id_type=MESH).wait_send()
+        gone = A.at[pl.ds(0, 7 * shard)]
+        pltpu.make_async_remote_copy(
+            src_ref=gone, dst_ref=gone, send_sem=act_send.at[0], recv_sem=act_recv.at[0],
+            device_id=(row, twin), device_id_type=MESH).wait_send()
+        strip(row).wait_send()
+
+    def factors(phase, carry):
+        first = phase == 0
+
+        def first_sums():
+            col_acc[...] = sums(squared)
+
+        def second_sums():
+            col_acc[...] = sums(strays)
+
+        pl.when(first)(first_sums)
+        pl.when(phase == 1)(second_sums)
+        col_sums = [col_acc[:, j * LANES:(j + 1) * LANES] for j in range(nc)]
         values = whole(functools.reduce(jnp.add, col_sums))
-        for lane, value in enumerate(beside):
+        for lane, value in enumerate(states_sums):
             values = jnp.where(lane_ids == lane + 1, value, values)
-        tot_part[phase] = jnp.broadcast_to(values, (1, LANES))
+        tot_part[phase] = values
         by_twin = exchange(phase, tot_part.at[phase], tot_got, core, to_twin, (tot_send, tot_recv))
         by_twin[0]()
         for j in range(nc):
@@ -349,69 +383,38 @@
         x_part[phase] = by_z[1]()
         by_x = exchange(phase, x_part.at[phase], x_got, x, to_x, (x_send, x_recv))
         by_x[0]()
-        meanwhile()
+        pl.when(first)(gather_drain)
         row_all = by_row[1]()
         col_all = by_x[1]()
         for one in (by_twin, by_z, by_row, by_x):
             one[2]()
         totals = by_all[1]()
-        return row_all, col_all, totals, by_all[2]
-
-    def down_rows(factors):
-        for i in range(nr):
-            row_scale[i * LANES:(i + 1) * LANES, :] = jnp.broadcast_to(factors[i:i + 1, :], (LANES, LANES)).T
-
-    def squared(at, j):
-        g = G[at, j * LANES:(j + 1) * LANES]
-        return g * g
-
-    def gather_drain():
-        for lane, (axis, sign) in enumerate(ring_to):
-            gone = sum(extent(m)[1] for m in sent if m[:2] == (axis, sign))
-            gone = B.at[pl.ds(0, gone)]
-            pltpu.make_async_remote_copy(
-                src_ref=gone, dst_ref=gone, send_sem=ring_send.at[lane], recv_sem=ring_recv.at[lane, 0],
-                device_id=(ring_to[axis, sign], col), device_id_type=MESH).wait_send()
-        gone = A.at[pl.ds(0, 7 * shard)]
-        pltpu.make_async_remote_copy(
-            src_ref=gone, dst_ref=gone, send_sem=act_send.at[0], recv_sem=act_recv.at[0],
-            device_id=(row, twin), device_id_type=MESH).wait_send()
-        strip(row).wait_send()
-
-    col_sum = sums(squared)
-    row_all, col_all, totals, drain0 = reduced(0, col_sum, states_sums, gather_drain)
-    total, row_state_sum, row_conf_sum = totals[:, 0:1], totals[:, 1:2] * (1.0 / C), totals[:, 2:3] * (1.0 / C)
-    spread = jnp.minimum(1.0, (full_rows * full_cols) / (total + 1e-06))
-    keep, fresh = second_decay, 1.0 - second_decay
-    row_new = keep * states[0] + fresh * (spread * row_all * (1.0 / full_cols) + tiny_moment)
-    col_new = keep * states[1] + fresh * (spread * col_all * (1.0 / full_rows) + tiny_moment)
-    row_mean = keep * (row_state_sum * (1.0 / full_rows)) + fresh * (
-        spread * total * (1.0 / (full_rows * full_cols)) + tiny_moment)
-    down_rows(lax.rsqrt(row_new))
-    packed[0] = row_new
-    packed[1] = col_new
-    col_scale = lax.rsqrt(col_new) * jnp.sqrt(spread * row_mean)
-
-    def strays(at, j):
-        here = (at, slice(j * LANES, (j + 1) * LANES))
-        direction = G[here] * row_scale[at, :] * col_scale[j:j + 1, :]
-        stray = direction - M[here]
-        M[here] = M[here] + (1.0 - first_decay) * stray
-        return stray * stray
-
-    col_sum = sums(strays)
-    row_all, col_all, totals, drain1 = reduced(1, col_sum, [], drain0)
-    total = totals[:, 0:1]
-    share = first_decay * first_decay
-    row_conf_new = keep * states[2] + fresh * (row_all * (share / full_cols) + tiny_confidence)
-    col_conf_new = keep * states[3] + fresh * (col_all * (share / full_rows) + tiny_confidence)
-    conf_mean = keep * (row_conf_sum * (1.0 / full_rows)) + fresh * (
-        total * (share / (full_rows * full_cols)) + tiny_confidence)
-    packed[2] = row_conf_new
-    packed[3] = col_conf_new
-    packed[4] = lax.rsqrt(row_conf_new)
-    packed[5] = lax.rsqrt(col_conf_new) * jnp.sqrt(conf_mean)
-    drain1()
+        total = totals[:, 0:1]
+        state_sum = jnp.where(first, totals[:, 1:2], totals[:, 2:3]) * (1.0 / C)
+        clipped = jnp.minimum(1.0, (full_rows * full_cols) / (total + 1e-06))
+        share = jnp.where(first, clipped, first_decay * first_decay)
+        tiny = jnp.where(first, tiny_moment, tiny_confidence)
+        keep, fresh = second_decay, 1.0 - second_decay
+        row_new = keep * states[2 * phase] + fresh * (share * row_all * (1.0 / full_cols) + tiny)
+        col_new = keep * states[2 * phase + 1] + fresh * (share * col_all * (1.0 / full_rows) + tiny)
+        mean = keep * (state_sum * (1.0 / full_rows)) + fresh * (
+            share * total * (1.0 / (full_rows * full_cols)) + tiny)
+        row_root = lax.rsqrt(row_new)
+
+        def turn():
+            for i in range(nr):
+                row_scale[i * LANES:(i + 1) * LANES, :] = jnp.broadcast_to(
+                    row_root[i:i + 1, :], (LANES, LANES)).T
+
+        pl.when(first)(turn)
+        packed[2 * phase] = row_new
+        packed[2 * phase + 1] = col_new
+        packed[4] = row_root
+        packed[5] = lax.rsqrt(col_new) * jnp.sqrt(jnp.where(first, clipped, 1.0) * mean)
+        by_all[2]()
+        return carry
+
+    lax.fori_loop(0, 2, factors, 0)
 
 
 def finish(M, packed, moment_out, update_out, row_out, col_out, row_conf_out, col_conf_out, U, sem, block_sem):
@@ -466,6 +469,7 @@
             pltpu.VMEM((tokens, cols), out_grads.dtype),
             pltpu.VMEM((rows, cols), F32),
             pltpu.VMEM((4, 8, LANES), F32),
+            pltpu.VMEM((8, cols), F32),
             pltpu.VMEM((rows, LANES), F32),
             pltpu.VMEM((rows, LANES), F32),
             pltpu.VMEM((2, 8, LANES), F32),

time: 79.8 us -> 79.9 us (level)
  no operation moved by 1% of the time
where the time goes in v11:
time: 79.9 us
  Pallas kernels  79.2 us (99%)
    pallas_call x1, Pallas kernels, on_device(): pl.pallas_call(functools.partial(kernel, R, C), out_shape=(pltpu.VMEM((ro...  76.1 us
    pallas_call x1, Pallas kernels, on_device(): pl.pallas_call(finish, out_shape=(big, big, by_row, by_col, by_row, by_co...  3.09 us

profile of v11, /device:TPU:1, one launch (start us, length us, event | category | flops | bytes accessed | tf_op | source)
XLA Modules:
  0.0 79.9 jit_solution(9268655293246482405)
XLA Ops:
  0.6 76.1 %came_step.1 = (f32[896,1024]{1,0:T(8,128)S(1)}, f32[6,8,128]{2,1,0:T(8,128)S(1)}) custom-call(bf16[512,896]{1,0:T(8,128)(2,1)} %acts.1, bf16[128,1024]{1,0:T(8,128)(2,1)} %grads.1, f32[896,1024]{1,0:T(8,128)} %moment.1, f32[7,128]{1,0:T(8,128)} %bitcast.8, f32[8,128]{1,0:T(8,128)} %bitcast.9, f32[7,128]{1,0:T(8,128)} %bitcast.10, f32[8,128]{1,0:T(8,128)} %bitcast.11), custom_call_target="tpu_custom_call" | custom-call | flops 7516192768 | bytes 31457280 | tf_op jit(solution)/shard_map/came_step/pallas_call | solution.py:462
  76.8 3.1 %finish.1 = (f32[896,1024]{1,0:T(8,128)}, f32[896,1024]{1,0:T(8,128)}, f32[7,128]{1,0:T(8,128)}, f32[8,128]{1,0:T(8,128)}, f32[7,128]{1,0:T(8,128)}, /*index=5*/f32[8,128]{1,0:T(8,128)}) custom-call(f32[896,1024]{1,0:T(8,128)S(1)} %get-tuple-element.14.M, f32[6,8,128]{2,1,0:T(8,128)S(1)} %get-tuple-element.15.packed), custom_call_target="tpu_custom_call" | custom-call | flops 1835008 | bytes 11010048 | tf_op jit(solution)/shard_map/finish/pallas_call | solution.py:496

commit v12 on v9

--- a/solution.py
+++ b/solution.py
@@ -281,6 +281,7 @@
         load.wait()
     col_part[...] = jnp.zeros_like(col_part)
     row_part[...] = jnp.zeros_like(row_part)
+    row_sums[...] = jnp.zeros_like(row_sums)
     lane_ids = lax.broadcasted_iota(jnp.int32, (1, LANES), 1)
     states_sums = [whole(states[k]) for k in (0, 2)]
     add_products(fours, FOURS_ORDER)
@@ -312,9 +313,14 @@
 
         return start, result, drain
 
-    def sums(block):
+    def turn_sums(phase, i):
+        turned = row_sums[part(i * LANES, LANES, LANES), :].T
+        row_part[phase, pl.ds(i, 1), :] = jnp.sum(turned, axis=0, keepdims=True)
+
+    def sums(phase, block):
         def rows_of(i, col_sum):
             at = part(i * LANES, LANES, LANES)
+            turn_sums(phase, jnp.maximum(i - 1, 0))
             row_sum = jnp.zeros((LANES, LANES), F32)
             col_sums = []
             for j in range(nc):
@@ -338,9 +344,7 @@
             col_part[phase, j:j + 1, :] = jnp.sum(col_sums[j], axis=0, keepdims=True)
         by_z = exchange(phase, col_part.at[phase], col_got, z, to_z, (col_send, col_recv))
         by_z[0]()
-        for i in range(nr):
-            turned = row_sums[i * LANES:(i + 1) * LANES, :].T
-            row_part[phase, i:i + 1, :] = jnp.sum(turned, axis=0, keepdims=True)
+        turn_sums(phase, nr - 1)
         by_row = exchange(phase, row_part.at[phase], row_got, col, to_col, (row_send, row_recv))
         by_row[0]()
         all_part[phase] = by_twin[1]()
@@ -378,7 +382,7 @@
             device_id=(row, twin), device_id_type=MESH).wait_send()
         strip(row).wait_send()
 
-    col_sum = sums(squared)
+    col_sum = sums(0, squared)
     row_all, col_all, totals, drain0 = reduced(0, col_sum, states_sums, gather_drain)
     total, row_state_sum, row_conf_sum = totals[:, 0:1], totals[:, 1:2] * (1.0 / C), totals[:, 2:3] * (1.0 / C)
     spread = jnp.minimum(1.0, (full_rows * full_cols) / (total + 1e-06))
@@ -399,7 +403,7 @@
         M[here] = M[here] + (1.0 - first_decay) * stray
         return stray * stray
 
-    col_sum = sums(strays)
+    col_sum = sums(1, strays)
     row_all, col_all, totals, drain1 = reduced(1, col_sum, [], drain0)
     total = totals[:, 0:1]
     share = first_decay * first_decay

time: 79.8 us -> 80.5 us (level)
  no operation moved by 1% of the time
where the time goes in v12:
time: 80.5 us
  Pallas kernels  79.8 us (99%)
    pallas_call x1, Pallas kernels, on_device(): pl.pallas_call(functools.partial(kernel, R, C), out_shape=(pltpu.VMEM((ro...  76.7 us
    pallas_call x1, Pallas kernels, on_device(): pl.pallas_call(finish, out_shape=(big, big, by_row, by_col, by_row, by_co...  3.09 us

profile of v12, /device:TPU:1, one launch (start us, length us, event | category | flops | bytes accessed | tf_op | source)
XLA Modules:
  0.0 80.5 jit_solution(15621831179229573215)
XLA Ops:
  0.6 76.7 %came_step.1 = (f32[896,1024]{1,0:T(8,128)S(1)}, f32[6,8,128]{2,1,0:T(8,128)S(1)}) custom-call(bf16[512,896]{1,0:T(8,128)(2,1)} %acts.1, bf16[128,1024]{1,0:T(8,128)(2,1)} %grads.1, f32[896,1024]{1,0:T(8,128)} %moment.1, f32[7,128]{1,0:T(8,128)} %bitcast.8, f32[8,128]{1,0:T(8,128)} %bitcast.9, f32[7,128]{1,0:T(8,128)} %bitcast.10, f32[8,128]{1,0:T(8,128)} %bitcast.11), custom_call_target="tpu_custom_call" | custom-call | flops 7516192768 | bytes 31457280 | tf_op jit(solution)/shard_map/came_step/pallas_call | solution.py:463
  77.4 3.1 %finish.1 = (f32[896,1024]{1,0:T(8,128)}, f32[896,1024]{1,0:T(8,128)}, f32[7,128]{1,0:T(8,128)}, f32[8,128]{1,0:T(8,128)}, f32[7,128]{1,0:T(8,128)}, /*index=5*/f32[8,128]{1,0:T(8,128)}) custom-call(f32[896,1024]{1,0:T(8,128)S(1)} %get-tuple-element.14.M, f32[6,8,128]{2,1,0:T(8,128)S(1)} %get-tuple-element.15.packed), custom_call_target="tpu_custom_call" | custom-call | flops 1835008 | bytes 11010048 | tf_op jit(solution)/shard_map/finish/pallas_call | solution.py:496
